TPU v7x, 256 devices: a whole 4x4x8 slice. The times are simulated.
256 devices in a mesh: wide: 32 (over z, x), tensor: 8 (over y, core).
Axes of the slice: x: 4, y: 4, z: 8, core: 2. Of those that a mesh axis runs over, the one named last changes fastest.
Arguments:
- queries: bfloat16 [4, 2048, 8192], P(None, 'wide', 'tensor'), may hold values from -6 to 6
- new_keys: bfloat16 [4, 2048, 1024], P(None, 'wide', 'tensor'), may hold values from -4.5 to 4.5
- new_values: bfloat16 [4, 2048, 1024], P(None, 'wide', 'tensor'), may hold values from -4.5 to 4.5
- suffix_keys: bfloat16 [2048, 64, 1024], P('wide', None, 'tensor'), may hold values from -4.5 to 4.5
- suffix_values: bfloat16 [2048, 64, 1024], P('wide', None, 'tensor'), may hold values from -4.5 to 4.5
- suffix_len: int32 [2048], P('wide'), may hold values from 1 to 64, 65536 in all
- prefix_keys: bfloat16 [64, 768, 1024], P('wide', None, 'tensor'), may hold values from -4.5 to 4.5
- prefix_values: bfloat16 [64, 768, 1024], P('wide', None, 'tensor'), may hold values from -4.5 to 4.5
- prefix_of: int32 [2048, 1], P('wide'), may hold values from 0 to 63; in each aligned block of 64 rows (0 to 63, 64 to 127, ...) at most 2 rows name the same one
- out_weight: bfloat16 [8192, 4096], P('tensor'), may hold values from -0.09375 to 0.09375
Outputs:
- projected: bfloat16 [4, 2048, 4096], P(None, 'wide', 'tensor')
Inputs may be any that keep to these rules, and one draw needn't show every extreme that they name: `prefix_of`: among the 64 requests of one index of wide, no prompt is named more than 2 times, and in some such block one prompt is named exactly 2 times; every prompt is named by some request. `suffix_len`: some request has exactly 64 valid rows.
All inputs are finite; a program needn't handle non-finite values. No bound on the sum of `suffix_len` on one device may be relied on, other than what follows from the above.
Results may differ from a plain program's by a relative error of at most 0.019.
Values may be sent and summed in bfloat16 or wider, within the bound.
A program may use at most 64 MiB of HBM per device.

v0:
```python
import jax
import jax.numpy as jnp
from jax import lax
from jax.sharding import PartitionSpec as P

HD = 128


def owner_attend(received, prefix_keys, prefix_values):
    slot_count, capacity, step_count, row_width = received.shape
    owned_count, prefix_length, kv_width = prefix_keys.shape
    kv_heads = kv_width // HD
    group_size = row_width // kv_width
    sources = slot_count // owned_count
    query_heads = received.reshape(
        sources, owned_count, capacity, step_count, kv_heads, group_size, HD
    )
    query_heads = query_heads.transpose(1, 4, 0, 2, 3, 5, 6).reshape(
        owned_count, kv_heads, sources * capacity * step_count * group_size, HD
    )
    head_keys = prefix_keys.reshape(owned_count, prefix_length, kv_heads, HD)
    head_values = prefix_values.reshape(owned_count, prefix_length, kv_heads, HD)
    scores = jnp.einsum(
        "pgqd,pkgd->pgqk", query_heads, head_keys, preferred_element_type=jnp.float32
    ) * HD ** (-0.5)
    highest = jnp.max(scores, axis=-1, keepdims=True)
    weights = jnp.exp(scores - highest)
    totals = jnp.sum(weights, axis=-1, keepdims=True)
    numerator = jnp.einsum(
        "pgqk,pkgd->pgqd",
        weights.astype(jnp.bfloat16),
        head_values,
        preferred_element_type=jnp.float32,
    )
    partial_out = (numerator / totals).reshape(
        owned_count, kv_heads, sources, capacity, step_count, group_size, HD
    )
    partial_out = partial_out.transpose(2, 0, 3, 4, 1, 5, 6).reshape(
        slot_count, capacity, step_count, row_width
    )
    log_total = (highest[..., 0] + jnp.log(totals[..., 0])).reshape(
        owned_count, kv_heads, sources, capacity, step_count, group_size
    )
    log_total = log_total.transpose(2, 0, 3, 4, 1, 5).reshape(
        slot_count, capacity, step_count, kv_heads * group_size
    )
    return (partial_out, log_total)


def body(
    queries,
    new_keys,
    new_values,
    suffix_keys,
    suffix_values,
    suffix_len,
    prefix_keys,
    prefix_values,
    prefix_of,
    out_weight,
):
    step_count, request_count, row_width = queries.shape
    kv_width = new_keys.shape[2]
    kv_heads = kv_width // HD
    group_size = row_width // kv_width
    past_count = suffix_keys.shape[1]
    prefix_count = prefix_keys.shape[0] * lax.axis_size("wide")
    slot_depth = max(2, (2 * request_count + prefix_count - 1) // prefix_count)
    scale = HD ** (-0.5)
    owner_ids = prefix_of[:, 0]
    member_table = (
        owner_ids[:, None] == jnp.arange(prefix_count, dtype=jnp.int32)[None, :]
    ).astype(jnp.int32)
    earlier = jnp.cumsum(member_table, axis=0) - member_table
    slot_index = owner_ids * slot_depth + jnp.sum(earlier * member_table, axis=1)
    outgoing = jnp.zeros((prefix_count * slot_depth, step_count, row_width), jnp.bfloat16)
    outgoing = (
        outgoing.at[slot_index]
        .set(queries.transpose(1, 0, 2))
        .reshape(prefix_count, slot_depth, step_count, row_width)
    )
    out_pieces = []
    log_pieces = []
    for step_index in range(step_count):
        partial_out, log_total = owner_attend(
            lax.all_to_all(
                outgoing[:, :, step_index : step_index + 1],
                "wide",
                split_axis=0,
                concat_axis=0,
                tiled=True,
            ),
            prefix_keys,
            prefix_values,
        )
        piece_out = lax.all_to_all(partial_out, "wide", split_axis=0, concat_axis=0, tiled=True)
        piece_log = lax.all_to_all(log_total, "wide", split_axis=0, concat_axis=0, tiled=True)
        out_pieces.append(piece_out)
        log_pieces.append(piece_log)
    back_out = jnp.concatenate(out_pieces, axis=2)
    back_log = jnp.concatenate(log_pieces, axis=2)
    back_out = back_out.reshape(prefix_count * slot_depth, step_count, row_width)[
        slot_index
    ].transpose(1, 0, 2)
    back_log = back_log.reshape(prefix_count * slot_depth, step_count, kv_heads * group_size)[
        slot_index
    ].transpose(1, 0, 2)
    prefix_out = back_out.reshape(step_count, request_count, kv_heads, group_size, HD)
    prefix_log = back_log.reshape(step_count, request_count, kv_heads, group_size)
    query_heads = queries.reshape(step_count, request_count, kv_heads, group_size, HD)
    local_keys = jnp.concatenate([suffix_keys, new_keys.transpose(1, 0, 2)], axis=1).reshape(
        request_count, past_count + step_count, kv_heads, HD
    )
    local_values = jnp.concatenate([suffix_values, new_values.transpose(1, 0, 2)], axis=1).reshape(
        request_count, past_count + step_count, kv_heads, HD
    )
    scores = (
        jnp.einsum("srgqd,rkgd->srgqk", query_heads, local_keys, preferred_element_type=jnp.float32)
        * scale
    )
    positions = jnp.arange(past_count + step_count, dtype=jnp.int32)
    step_ids = jnp.arange(step_count, dtype=jnp.int32)
    visible = jnp.where(
        positions[None, None, :] < past_count,
        positions[None, None, :] < suffix_len[None, :, None],
        positions[None, None, :] - past_count <= step_ids[:, None, None],
    )
    scores = jnp.where(visible[:, :, None, None, :], scores, -jnp.inf)
    highest = jnp.max(scores, axis=-1, keepdims=True)
    weights = jnp.exp(scores - highest)
    totals = jnp.sum(weights, axis=-1, keepdims=True)
    numerator = jnp.einsum(
        "srgqk,rkgd->srgqd",
        weights.astype(jnp.bfloat16),
        local_values,
        preferred_element_type=jnp.float32,
    )
    local_out = numerator / totals
    local_log = highest[..., 0] + jnp.log(totals[..., 0])
    joint_max = jnp.maximum(prefix_log, local_log)
    prefix_weight = jnp.exp(prefix_log - joint_max)[..., None]
    local_weight = jnp.exp(local_log - joint_max)[..., None]
    merged = (prefix_weight * prefix_out + local_weight * local_out) / (
        prefix_weight + local_weight
    )
    attention = merged.reshape(step_count * request_count, row_width).astype(jnp.bfloat16)
    share_width = out_weight.shape[1] // lax.axis_size("tensor")
    head_terms = jnp.dot(attention, out_weight, preferred_element_type=jnp.float32)
    summed = lax.psum(head_terms.astype(jnp.bfloat16), "tensor").astype(jnp.float32)
    mine = lax.dynamic_slice_in_dim(summed, lax.axis_index("tensor") * share_width, share_width, 1)
    return mine.astype(jnp.bfloat16).reshape(step_count, request_count, share_width)


def solution(mesh):
    return jax.shard_map(
        body,
        mesh=mesh,
        in_specs=(
            P(None, "wide", "tensor"),
            P(None, "wide", "tensor"),
            P(None, "wide", "tensor"),
            P("wide", None, "tensor"),
            P("wide", None, "tensor"),
            P("wide"),
            P("wide", None, "tensor"),
            P("wide", None, "tensor"),
            P("wide", None),
            P("tensor", None),
        ),
        out_specs=P(None, "wide", "tensor"),
        check_vma=False,
    )
```

profile of v0, /device:TPU:1, one launch (start us, length us, event | category | flops | bytes accessed | tf_op | source)
XLA Modules:
  0.0 324.0 jit_solution(1628878346993515274)
XLA Ops:
  8.9 1.4 copy.189
  10.7 2.4 scatter_fusion
  13.1 1.6 fusion.63
  14.7 1.0 copy.232
  15.6 11.9 %all-to-all-start = ((bf16[64,2,1,1024]{3,1,2,0:T(2,128)(2,1)}), bf16[64,2,1,1024]{3,1,2,0:T(2,128)(2,1)S(1)}, u32[]{:S(2)}, u32[]{:S(2)}) async-start(bf16[64,2,1,1024]{3,1,2,0:T(2,128)(2,1)} %copy.232), calls=%async_computation | async-start | bytes 524288 | tf_op jit(solution)/shard_map/all_to_all | solution.py:86
  27.5 1.0 copy.233
  28.5 10.2 %all-to-all-done = bf16[64,2,1,1024]{3,1,2,0:T(2,128)(2,1)S(1)} async-done(((bf16[64,2,1,1024]{3,1,2,0:T(2,128)(2,1)}), bf16[64,2,1,1024]{3,1,2,0:T(2,128)(2,1)S(1)}, u32[]{:S(2)}, u32[]{:S(2)}) %all-to-all-start) | async-done | bytes 262176 | tf_op jit(solution)/shard_map/all_to_all | solution.py:86
  38.7 4.8 %all-to-all-start.2 = ((bf16[64,2,1,1024]{3,1,2,0:T(2,128)(2,1)}), bf16[64,2,1,1024]{3,1,2,0:T(2,128)(2,1)S(1)}, u32[]{:S(2)}, u32[]{:S(2)}) async-start(bf16[64,2,1,1024]{3,1,2,0:T(2,128)(2,1)} %copy.233), calls=%async_computation.2 | async-start | bytes 524288 | tf_op jit(solution)/shard_map/all_to_all | solution.py:86
  43.5 1.0 copy.234
  44.4 9.4 %all-to-all-done.2 = bf16[64,2,1,1024]{3,1,2,0:T(2,128)(2,1)S(1)} async-done(((bf16[64,2,1,1024]{3,1,2,0:T(2,128)(2,1)}), bf16[64,2,1,1024]{3,1,2,0:T(2,128)(2,1)S(1)}, u32[]{:S(2)}, u32[]{:S(2)}) %all-to-all-start.2) | async-done | bytes 262176 | tf_op jit(solution)/shard_map/all_to_all | solution.py:86
  53.9 4.6 %all-to-all-start.4 = ((bf16[64,2,1,1024]{3,1,2,0:T(2,128)(2,1)}), bf16[64,2,1,1024]{3,1,2,0:T(2,128)(2,1)S(1)}, u32[]{:S(2)}, u32[]{:S(2)}) async-start(bf16[64,2,1,1024]{3,1,2,0:T(2,128)(2,1)} %copy.234), calls=%async_computation.4 | async-start | bytes 524288 | tf_op jit(solution)/shard_map/all_to_all | solution.py:86
  58.5 1.0 copy.235
  60.1 8.9 %all-to-all-done.4 = bf16[64,2,1,1024]{3,1,2,0:T(2,128)(2,1)S(1)} async-done(((bf16[64,2,1,1024]{3,1,2,0:T(2,128)(2,1)}), bf16[64,2,1,1024]{3,1,2,0:T(2,128)(2,1)S(1)}, u32[]{:S(2)}, u32[]{:S(2)}) %all-to-all-start.4) | async-done | bytes 262176 | tf_op jit(solution)/shard_map/all_to_all | solution.py:86
  68.9 3.9 %all-to-all-start.6 = ((bf16[64,2,1,1024]{3,1,2,0:T(2,128)(2,1)}), bf16[64,2,1,1024]{3,1,2,0:T(2,128)(2,1)S(1)}, u32[]{:S(2)}, u32[]{:S(2)}) async-start(bf16[64,2,1,1024]{3,1,2,0:T(2,128)(2,1)} %copy.235), calls=%async_computation.6 | async-start | bytes 524288 | tf_op jit(solution)/shard_map/all_to_all | solution.py:86
  73.1 2.3 multiply_reduce_fusion.3
  75.4 2.2 multiply_reduce_fusion.2
  77.6 2.2 multiply_reduce_fusion.1
  79.9 3.3 %all-to-all-done.6 = bf16[64,2,1,1024]{3,1,2,0:T(2,128)(2,1)S(1)} async-done(((bf16[64,2,1,1024]{3,1,2,0:T(2,128)(2,1)}), bf16[64,2,1,1024]{3,1,2,0:T(2,128)(2,1)S(1)}, u32[]{:S(2)}, u32[]{:S(2)}) %all-to-all-start.6) | async-done | bytes 262176 | tf_op jit(solution)/shard_map/all_to_all | solution.py:86
  84.1 2.6 fusion.1
  87.9 1.5 add.97
  89.4 0.9 copy.193
  91.0 6.2 %all-to-all-start.1 = ((f32[64,2,1,8]{3,1,2,0:T(2,128)}), f32[64,2,1,8]{3,1,2,0:T(2,128)}, u32[]{:S(2)}, u32[]{:S(2)}) async-start(f32[64,2,1,8]{3,1,2,0:T(2,128)} %copy.194), calls=%async_computation.1 | async-start | bytes 131072 | tf_op jit(solution)/shard_map/all_to_all | solution.py:97
  97.2 2.7 fusion.3
  100.0 1.3 fusion.5
  101.3 1.3 fusion.7
  103.3 1.5 add.99
  104.7 0.9 copy.198
  106.3 9.1 %all-to-all-start.3 = ((f32[64,2,1,8]{3,1,2,0:T(2,128)}), f32[64,2,1,8]{3,1,2,0:T(2,128)}, u32[]{:S(2)}, u32[]{:S(2)}) async-start(f32[64,2,1,8]{3,1,2,0:T(2,128)} %copy.199), calls=%async_computation.3 | async-start | bytes 131072 | tf_op jit(solution)/shard_map/all_to_all | solution.py:97
  115.4 1.3 log_add_fusion.2
  116.7 1.5 add.101
  118.1 0.9 copy.203
  119.7 4.5 %all-to-all-done.3 = f32[64,2,1,8]{3,1,2,0:T(2,128)} async-done(((f32[64,2,1,8]{3,1,2,0:T(2,128)}), f32[64,2,1,8]{3,1,2,0:T(2,128)}, u32[]{:S(2)}, u32[]{:S(2)}) %all-to-all-start.3) | async-done | bytes 4128 | tf_op jit(solution)/shard_map/all_to_all | solution.py:97
  124.2 4.8 %all-to-all-start.5 = ((f32[64,2,1,8]{3,1,2,0:T(2,128)}), f32[64,2,1,8]{3,1,2,0:T(2,128)}, u32[]{:S(2)}, u32[]{:S(2)}) async-start(f32[64,2,1,8]{3,1,2,0:T(2,128)} %copy.204), calls=%async_computation.5 | async-start | bytes 131072 | tf_op jit(solution)/shard_map/all_to_all | solution.py:97
  129.0 1.3 log_add_fusion.1
  130.3 1.5 add.103
  131.8 0.9 copy.208
  133.3 4.5 %all-to-all-done.5 = f32[64,2,1,8]{3,1,2,0:T(2,128)} async-done(((f32[64,2,1,8]{3,1,2,0:T(2,128)}), f32[64,2,1,8]{3,1,2,0:T(2,128)}, u32[]{:S(2)}, u32[]{:S(2)}) %all-to-all-start.5) | async-done | bytes 4128 | tf_op jit(solution)/shard_map/all_to_all | solution.py:97
  137.8 4.8 %all-to-all-start.7 = ((f32[64,2,1,8]{3,1,2,0:T(2,128)}), f32[64,2,1,8]{3,1,2,0:T(2,128)}, u32[]{:S(2)}, u32[]{:S(2)}) async-start(f32[64,2,1,8]{3,1,2,0:T(2,128)} %copy.209), calls=%async_computation.7 | async-start | bytes 131072 | tf_op jit(solution)/shard_map/all_to_all | solution.py:97
  142.6 2.8 fusion.26
  145.4 0.9 copy.218
  146.3 5.1 %all-to-all-done.7 = f32[64,2,1,8]{3,1,2,0:T(2,128)} async-done(((f32[64,2,1,8]{3,1,2,0:T(2,128)}), f32[64,2,1,8]{3,1,2,0:T(2,128)}, u32[]{:S(2)}, u32[]{:S(2)}) %all-to-all-start.7) | async-done | bytes 4128 | tf_op jit(solution)/shard_map/all_to_all | solution.py:97
  151.4 4.6 %all-to-all-start.8 = ((f32[64,2,1,1024]{3,2,1,0:T(1,128)}), f32[64,2,1,1024]{3,2,1,0:T(1,128)}, u32[]{:S(2)}, u32[]{:S(2)}) async-start(f32[64,2,1,1024]{3,2,1,0:T(1,128)} %bitcast.138), calls=%async_computation.8 | async-start | bytes 1048576 | tf_op jit(solution)/shard_map/all_to_all | solution.py:96
  156.0 2.8 fusion.29
  158.8 0.9 copy.219
  159.7 9.2 %all-to-all-done.8 = f32[64,2,1,1024]{3,2,1,0:T(1,128)} async-done(((f32[64,2,1,1024]{3,2,1,0:T(1,128)}), f32[64,2,1,1024]{3,2,1,0:T(1,128)}, u32[]{:S(2)}, u32[]{:S(2)}) %all-to-all-start.8) | async-done | bytes 524320 | tf_op jit(solution)/shard_map/all_to_all | solution.py:96
  169.0 4.6 %all-to-all-start.9 = ((f32[64,2,1,1024]{3,2,1,0:T(1,128)}), f32[64,2,1,1024]{3,2,1,0:T(1,128)}, u32[]{:S(2)}, u32[]{:S(2)}) async-start(f32[64,2,1,1024]{3,2,1,0:T(1,128)} %bitcast.139), calls=%async_computation.9 | async-start | bytes 1048576 | tf_op jit(solution)/shard_map/all_to_all | solution.py:96
  173.6 2.8 fusion.32
  176.4 0.9 copy.220
  177.3 9.2 %all-to-all-done.9 = f32[64,2,1,1024]{3,2,1,0:T(1,128)} async-done(((f32[64,2,1,1024]{3,2,1,0:T(1,128)}), f32[64,2,1,1024]{3,2,1,0:T(1,128)}, u32[]{:S(2)}, u32[]{:S(2)}) %all-to-all-start.9) | async-done | bytes 524320 | tf_op jit(solution)/shard_map/all_to_all | solution.py:96
  186.5 4.6 %all-to-all-start.10 = ((f32[64,2,1,1024]{3,2,1,0:T(1,128)}), f32[64,2,1,1024]{3,2,1,0:T(1,128)}, u32[]{:S(2)}, u32[]{:S(2)}) async-start(f32[64,2,1,1024]{3,2,1,0:T(1,128)} %bitcast.137), calls=%async_computation.10 | async-start | bytes 1048576 | tf_op jit(solution)/shard_map/all_to_all | solution.py:96
  192.9 1.8 fusion.35
  194.7 0.9 copy.221
  195.6 8.1 %all-to-all-done.10 = f32[64,2,1,1024]{3,2,1,0:T(1,128)} async-done(((f32[64,2,1,1024]{3,2,1,0:T(1,128)}), f32[64,2,1,1024]{3,2,1,0:T(1,128)}, u32[]{:S(2)}, u32[]{:S(2)}) %all-to-all-start.10) | async-done | bytes 524320 | tf_op jit(solution)/shard_map/all_to_all | solution.py:96
  203.7 4.1 %all-to-all-start.11 = ((f32[64,2,1,1024]{3,2,1,0:T(1,128)}), f32[64,2,1,1024]{3,2,1,0:T(1,128)S(1)}, u32[]{:S(2)}, u32[]{:S(2)}) async-start(f32[64,2,1,1024]{3,2,1,0:T(1,128)} %bitcast.39), calls=%async_computation.11 | async-start | bytes 1048576 | tf_op jit(solution)/shard_map/all_to_all | solution.py:96
  208.9 1.2 copy.236
  210.1 2.1 fusion.64
  213.9 1.1 pad_maximum_fusion.1
  218.2 2.5 all-to-all-done.11
  220.7 3.3 %pad_maximum_fusion = f32[64,2,4,1024]{3,2,1,0:T(4,128)S(1)} fusion(f32[64,2,1,1024]{3,2,1,0:T(1,128)S(1)} %all-to-all-done.11, f32[64,2,1,1024]{3,2,1,0:T(1,128)} %all-to-all-done.10, f32[64,2,1,1024]{3,2,1,0:T(1,128)} %all-to-all-done.9, f32[64,2,1,1024]{3,2,1,0:T(1,128)} %all-to-all-done.8), kind=kLoop, calls=%fused_computation.20 | loop fusion | flops 1572864 | bytes 4194304 | tf_op jit(solution)/shard_map/concatenate | solution.py:100
  224.1 1.2 gather_fusion.1
  225.7 3.2 divide_convert_fusion
  228.9 7.0 %convolution_convert_fusion = bf16[256,4096]{1,0:T(8,128)(2,1)} fusion(bf16[1024,4096]{1,0:T(8,128)(2,1)} %param.19, bf16[32,8,8,128]{3,2,1,0:T(8,128)(2,1)S(1)} %bitcast.154), kind=kOutput, calls=%fused_computation.3 | convolution fusion | flops 2148532224 | bytes 11010048 | tf_op jit(solution)/shard_map/dot_general | solution.py:148
  236.0 79.5 %all-reduce.2.cloned.1.call-done = bf16[256,4096]{1,0:T(8,128)(2,1)} async-done(((bf16[256,4096]{1,0:T(8,128)(2,1)}), bf16[256,4096]{1,0:T(8,128)(2,1)}) %all-reduce.2.cloned.1.call-update) | async-done | bytes 2097168 | tf_op jit(solution)/shard_map/psum | solution.py:149
  315.5 1.7 convert_convert_fusion
  (72 shorter events, 17.2 us)
Async XLA Ops:
  6.5 66.6 %copy-start = (bf16[2,768,128]{2,1,0:T(8,128)(2,1)S(1)}, bf16[2,768,128]{2,1,0:T(8,128)(2,1)}, u32[]{:S(2)}) copy-start(bf16[2,768,128]{2,1,0:T(8,128)(2,1)} %param.16) | copy-start | bytes 1179652
  8.9 4.2 %copy-start.10 = (s32[64]{0:T(128)}, s32[64]{0:T(128)S(1)}, u32[]{:S(2)}) copy-start(s32[64]{0:T(128)S(1)} %fusion.53) | copy-start | bytes 772
  15.6 23.1 %all-to-all-start = ((bf16[64,2,1,1024]{3,1,2,0:T(2,128)(2,1)}), bf16[64,2,1,1024]{3,1,2,0:T(2,128)(2,1)S(1)}, u32[]{:S(2)}, u32[]{:S(2)}) async-start(bf16[64,2,1,1024]{3,1,2,0:T(2,128)(2,1)} %copy.232), calls=%async_computation | async-start | bytes 524288 | tf_op jit(solution)/shard_map/all_to_all | solution.py:86
  38.7 15.2 %all-to-all-start.2 = ((bf16[64,2,1,1024]{3,1,2,0:T(2,128)(2,1)}), bf16[64,2,1,1024]{3,1,2,0:T(2,128)(2,1)S(1)}, u32[]{:S(2)}, u32[]{:S(2)}) async-start(bf16[64,2,1,1024]{3,1,2,0:T(2,128)(2,1)} %copy.233), calls=%async_computation.2 | async-start | bytes 524288 | tf_op jit(solution)/shard_map/all_to_all | solution.py:86
  53.9 15.1 %all-to-all-start.4 = ((bf16[64,2,1,1024]{3,1,2,0:T(2,128)(2,1)}), bf16[64,2,1,1024]{3,1,2,0:T(2,128)(2,1)S(1)}, u32[]{:S(2)}, u32[]{:S(2)}) async-start(bf16[64,2,1,1024]{3,1,2,0:T(2,128)(2,1)} %copy.234), calls=%async_computation.4 | async-start | bytes 524288 | tf_op jit(solution)/shard_map/all_to_all | solution.py:86
  68.9 14.2 %all-to-all-start.6 = ((bf16[64,2,1,1024]{3,1,2,0:T(2,128)(2,1)}), bf16[64,2,1,1024]{3,1,2,0:T(2,128)(2,1)S(1)}, u32[]{:S(2)}, u32[]{:S(2)}) async-start(bf16[64,2,1,1024]{3,1,2,0:T(2,128)(2,1)} %copy.235), calls=%async_computation.6 | async-start | bytes 524288 | tf_op jit(solution)/shard_map/all_to_all | solution.py:86
  86.7 0.6 copy-start.9
  91.0 15.3 %all-to-all-start.1 = ((f32[64,2,1,8]{3,1,2,0:T(2,128)}), f32[64,2,1,8]{3,1,2,0:T(2,128)}, u32[]{:S(2)}, u32[]{:S(2)}) async-start(f32[64,2,1,8]{3,1,2,0:T(2,128)} %copy.194), calls=%async_computation.1 | async-start | bytes 131072 | tf_op jit(solution)/shard_map/all_to_all | solution.py:97
  97.2 2.8 copy-start.1
  99.9 2.7 copy-start.8
  106.3 17.9 %all-to-all-start.3 = ((f32[64,2,1,8]{3,1,2,0:T(2,128)}), f32[64,2,1,8]{3,1,2,0:T(2,128)}, u32[]{:S(2)}, u32[]{:S(2)}) async-start(f32[64,2,1,8]{3,1,2,0:T(2,128)} %copy.199), calls=%async_computation.3 | async-start | bytes 131072 | tf_op jit(solution)/shard_map/all_to_all | solution.py:97
  124.2 13.6 %all-to-all-start.5 = ((f32[64,2,1,8]{3,1,2,0:T(2,128)}), f32[64,2,1,8]{3,1,2,0:T(2,128)}, u32[]{:S(2)}, u32[]{:S(2)}) async-start(f32[64,2,1,8]{3,1,2,0:T(2,128)} %copy.204), calls=%async_computation.5 | async-start | bytes 131072 | tf_op jit(solution)/shard_map/all_to_all | solution.py:97
  137.8 13.6 %all-to-all-start.7 = ((f32[64,2,1,8]{3,1,2,0:T(2,128)}), f32[64,2,1,8]{3,1,2,0:T(2,128)}, u32[]{:S(2)}, u32[]{:S(2)}) async-start(f32[64,2,1,8]{3,1,2,0:T(2,128)} %copy.209), calls=%async_computation.7 | async-start | bytes 131072 | tf_op jit(solution)/shard_map/all_to_all | solution.py:97
  151.4 17.5 %all-to-all-start.8 = ((f32[64,2,1,1024]{3,2,1,0:T(1,128)}), f32[64,2,1,1024]{3,2,1,0:T(1,128)}, u32[]{:S(2)}, u32[]{:S(2)}) async-start(f32[64,2,1,1024]{3,2,1,0:T(1,128)} %bitcast.138), calls=%async_computation.8 | async-start | bytes 1048576 | tf_op jit(solution)/shard_map/all_to_all | solution.py:96
  169.0 17.5 %all-to-all-start.9 = ((f32[64,2,1,1024]{3,2,1,0:T(1,128)}), f32[64,2,1,1024]{3,2,1,0:T(1,128)}, u32[]{:S(2)}, u32[]{:S(2)}) async-start(f32[64,2,1,1024]{3,2,1,0:T(1,128)} %bitcast.139), calls=%async_computation.9 | async-start | bytes 1048576 | tf_op jit(solution)/shard_map/all_to_all | solution.py:96
  173.6 19.3 %copy-start.7 = (f32[2,512]{1,0:T(2,128)S(1)}, f32[2,512]{1,0:T(2,128)}, u32[]{:S(2)}) copy-start(f32[2,512]{1,0:T(2,128)} %fusion.7) | copy-start | bytes 12292
  186.5 17.2 %all-to-all-start.10 = ((f32[64,2,1,1024]{3,2,1,0:T(1,128)}), f32[64,2,1,1024]{3,2,1,0:T(1,128)}, u32[]{:S(2)}, u32[]{:S(2)}) async-start(f32[64,2,1,1024]{3,2,1,0:T(1,128)} %bitcast.137), calls=%async_computation.10 | async-start | bytes 1048576 | tf_op jit(solution)/shard_map/all_to_all | solution.py:96
  194.7 15.3 %copy-start.5 = (bf16[4,64,128]{2,1,0:T(8,128)(2,1)S(1)}, bf16[4,64,128]{2,1,0:T(8,128)(2,1)}, u32[]{:S(2)}) copy-start(bf16[4,64,128]{2,1,0:T(8,128)(2,1)} %param.11) | copy-start | bytes 196612
  203.7 17.0 %all-to-all-start.11 = ((f32[64,2,1,1024]{3,2,1,0:T(1,128)}), f32[64,2,1,1024]{3,2,1,0:T(1,128)S(1)}, u32[]{:S(2)}, u32[]{:S(2)}) async-start(f32[64,2,1,1024]{3,2,1,0:T(1,128)} %bitcast.39), calls=%async_computation.11 | async-start | bytes 1048576 | tf_op jit(solution)/shard_map/all_to_all | solution.py:96
  207.9 107.6 %all-reduce.2.cloned.1.call-start = ((), (), s32[]{:S(2)}) async-start(), calls=%async_computation.12 | async-start | bytes 4194304 | tf_op jit(solution)/shard_map/psum | solution.py:149
  208.8 4.3 %copy-start.6 = (bf16[4,64,128]{2,1,0:T(8,128)(2,1)S(1)}, bf16[4,64,128]{2,1,0:T(8,128)(2,1)}, u32[]{:S(2)}) copy-start(bf16[4,64,128]{2,1,0:T(8,128)(2,1)} %param.12) | copy-start | bytes 196612
  208.8 5.0 %copy-start.11 = (s32[64]{0:T(128)S(1)}, s32[64]{0:T(128)}, u32[]{:S(2)}) copy-start(s32[64]{0:T(128)} %copy-done.10) | copy-start | bytes 772
  212.2 1.7 copy-start.3
  212.2 6.0 %copy-start.2 = (f32[4,64,1,8,68]{4,3,0,1,2:T(8,128)}, f32[4,64,1,8,68]{4,3,0,1,2:T(8,128)S(1)}, u32[]{:S(2)}) copy-start(f32[4,64,1,8,68]{4,3,0,1,2:T(8,128)S(1)} %get-tuple-element.21) | copy-start | bytes 1671172
  213.1 0.8 copy-start.4
Sparse Core Ops, SparseCore 0:
  236.1 79.3 all-reduce.1
where the time goes:
time: 327 us; the launch traced here: 324 us
  waiting for transfers between devices  155 us (47%)
  starting transfers between devices  68.3 us (21%)
  local copies, waits for them, and re-layouts  34 us (10%)
  matrix products  29.8 us (9%)
  other arithmetic  23.5 us (7%)
  between operations  13.9 us (4%)
    psum x1, waiting for transfers between devices, body(): lax.psum(head_terms.astype(jnp.bfloat16), 'tensor').astype(jnp.float32)  79.5 us
    all_to_all x4, waiting for transfers between devices, body(): lax.all_to_all(outgoing[:, :, step_index:step_index + 1], 'wide', split_a...  31.8 us
    all_to_all x4, waiting for transfers between devices, body(): lax.all_to_all(partial_out, 'wide', split_axis=0, concat_axis=0, tiled=True)  29.1 us
    all_to_all x4, starting transfers between devices, body(): lax.all_to_all(outgoing[:, :, step_index:step_index + 1], 'wide', split_a...  25.1 us
    all_to_all x4, starting transfers between devices, body(): lax.all_to_all(log_total, 'wide', split_axis=0, concat_axis=0, tiled=True)  24.9 us
    all_to_all x4, starting transfers between devices, body(): lax.all_to_all(partial_out, 'wide', split_axis=0, concat_axis=0, tiled=True)  18 us
    all_to_all x4, waiting for transfers between devices, body(): lax.all_to_all(log_total, 'wide', split_axis=0, concat_axis=0, tiled=True)  14.1 us
    dot_general x4, matrix products, owner_attend(): jnp.einsum('pgqk,pkgd->pgqd', weights.astype(jnp.bfloat16), head_values,...  10.2 us
  transfers between devices with their start and end apart: 13, of which 12 were waited for; matrix products, arithmetic and copies ran while one was open for 16% of the time, Pallas kernels for 0%

commit v1 on v0

v1 whole, which is shorter than its diff:
```python
import functools

import jax
import jax.numpy as jnp
from jax import lax
from jax.experimental import pallas as pl
from jax.experimental.pallas import tpu as pltpu
from jax.sharding import PartitionSpec as P

MESH = pl.DeviceIdType.MESH
HD = 128
NZ, NX, NY = 8, 4, 4
NW = NZ * NX
STEPS, REQ, HL = 4, 64, 8
PRE, SUF = 768, 64
ROWS = HL * REQ
SCALE = HD ** (-0.5)
LOG2E = 1.4426950408889634
BLOCK = 8
LKEYS = BLOCK * SUF
DOUT = 4096
SHARE = 512
F32, BF16, I32 = jnp.float32, jnp.bfloat16, jnp.int32


def dot(a, b):
    return lax.dot_general(a, b, (((1,), (0,)), ((), ())), preferred_element_type=F32)


def dot_t(a, b):
    return lax.dot_general(a, b, (((1,), (1,)), ((), ())), preferred_element_type=F32)


def kernel(
    q_hbm, pof_row, pof_col, len_col, nk_hbm, nv_hbm, sk_hbm, sv_hbm, pk_hbm, pv_hbm, w_hbm,
    out_hbm,
    q, nk, nv, sk, sv, pk, pv, w, vones, qf, nkf, nvf, kloc, vloc,
    spread, gather, q_send, q_recv, r_send, r_recv, l_send, l_recv,
    loc_out, loc_log, attn, proj, c_recv, y_send, y_recv, out_v,
    in_sems, out_sems, qs, qr, rs, rr, ls, lr, cs, cr, ys, yr,
):
    me_w, me_t = lax.axis_index("wide"), lax.axis_index("tensor")
    z, x = me_w // NX, me_w % NX
    y, c = me_t // 2, me_t % 2

    def offset(i):
        zi = i // NX
        half = (zi + 1) // 2
        dz = lax.rem(jnp.where(lax.rem(zi, 2) == 1, half, NZ - half), NZ)
        return dz, lax.rem(i, NX)

    def ahead(dz, dx):
        return (lax.rem(z + dz, NZ) * NX + lax.rem(x + dx, NX), me_t)

    def behind(dz, dx):
        return (lax.rem(z + NZ - dz, NZ) * NX + lax.rem(x + NX - dx, NX), me_t)

    def across(dy):
        return (me_w, lax.rem(y + dy, NY) * 2 + c)

    other = (me_w, y * 2 + 1 - c)

    loads = [
        pltpu.make_async_copy(src, dst, in_sems.at[n])
        for n, (src, dst) in enumerate(
            [(q_hbm, q), (pk_hbm, pk), (pv_hbm, pv), (nk_hbm, nk), (nv_hbm, nv),
             (sk_hbm, sk), (sv_hbm, sv), (w_hbm, w)]
        )
    ]
    for load in loads:
        load.start()

    barrier = pltpu.get_barrier_semaphore()

    def greet(i, carry):
        pl.semaphore_signal(barrier, inc=1, device_id=ahead(*offset(i)), device_id_type=MESH)
        return carry

    lax.fori_loop(1, NW, greet, 0)
    for dy in range(1, NY):
        pl.semaphore_signal(barrier, inc=1, device_id=across(dy), device_id_type=MESH)
    pl.semaphore_signal(barrier, inc=1, device_id=other, device_id_type=MESH)

    def slot_of(pof, rank):
        owner = lax.shift_right_logical(pof, 1)
        dz = lax.bitwise_and(lax.shift_right_logical(owner, 2) - z + NZ, NZ - 1)
        dx = lax.bitwise_and(lax.bitwise_and(owner, NX - 1) - x + NX, NX - 1)
        return dz * NX + dx, lax.bitwise_and(pof, 1), rank

    prow = pof_row[...]
    pcol = pof_col[...]
    same = pcol[:REQ] == prow
    before = lax.broadcasted_iota(I32, (REQ, ROWS), 0) < lax.bitwise_and(
        lax.broadcasted_iota(I32, (REQ, ROWS), 1), REQ - 1
    )
    rank_row = jnp.sum(jnp.where(same & before, 1, 0), axis=0, keepdims=True)
    o_row, p_row, k_row = slot_of(prow, rank_row)
    head_row = lax.shift_right_logical(lax.broadcasted_iota(I32, (1, ROWS), 1), 6)
    key_row = (o_row * HL + head_row) * 2 + k_row
    slot_rows = lax.broadcasted_iota(I32, (ROWS, ROWS), 0)
    for p in range(2):
        hit = slot_rows == jnp.where(p_row == p, key_row, -1)
        spread[p] = jnp.where(hit, 1.0, 0.0).astype(BF16)

    loads[0].wait()

    def dispatch(s):
        stacked = jnp.concatenate([q[s, :, h * HD:(h + 1) * HD] for h in range(HL)], axis=0)
        for p in range(2):
            placed = dot(spread[p], stacked).astype(BF16).reshape(NW, 2 * HL, HD)
            q_send[s, :, :, p * HD:(p + 1) * HD] = placed
            q_recv[s, 0, :, p * HD:(p + 1) * HD] = placed[0]

    def send_queries(s):
        def one(i, carry):
            dz, dx = offset(NW - i)
            o = dz * NX + dx
            pltpu.make_async_remote_copy(
                src_ref=q_send.at[s, o], dst_ref=q_recv.at[s, o], send_sem=qs.at[s],
                recv_sem=qr.at[s], device_id=ahead(dz, dx), device_id_type=MESH,
            ).start()
            return carry

        lax.fori_loop(1, NW, one, 0)

    def send_results(s):
        def one(i, carry):
            dz, dx = offset(NW - i)
            o = dz * NX + dx
            pltpu.make_async_remote_copy(
                src_ref=r_send.at[s, o], dst_ref=r_recv.at[s, o], send_sem=rs.at[s],
                recv_sem=rr.at[s], device_id=behind(dz, dx), device_id_type=MESH,
            ).start()
            pltpu.make_async_remote_copy(
                src_ref=l_send.at[s, o], dst_ref=l_recv.at[s, o], send_sem=ls.at[s],
                recv_sem=lr.at[s], device_id=behind(dz, dx), device_id_type=MESH,
            ).start()
            return carry

        lax.fori_loop(1, NW, one, 0)

    def await_all(ref, sem):
        pltpu.make_async_copy(ref, ref, sem).wait()

    dispatch(0)
    pl.semaphore_wait(barrier, NW - 1 + NY - 1 + 1)
    send_queries(0)
    dispatch(1)
    send_queries(1)
    dispatch(2)
    dispatch(3)

    same_c = pcol == prow[:, :REQ]
    before_c = lax.broadcasted_iota(I32, (ROWS, REQ), 1) < lax.bitwise_and(
        lax.broadcasted_iota(I32, (ROWS, REQ), 0), REQ - 1
    )
    rank_col = jnp.sum(jnp.where(same_c & before_c, 1, 0), axis=1, keepdims=True)
    o_col, p_col, k_col = slot_of(pcol, rank_col)
    head_col = lax.shift_right_logical(lax.broadcasted_iota(I32, (ROWS, 1), 0), 6)
    key_col = (o_col * HL + head_col) * 2 + k_col
    slot_cols = lax.broadcasted_iota(I32, (ROWS, ROWS), 1)
    for p in range(2):
        hit = slot_cols == jnp.where(p_col == p, key_col, -1)
        gather[p] = jnp.where(hit, 1.0, 0.0).astype(BF16)
    loads[1].wait()
    loads[2].wait()
    vones[:, :, :HD] = pv[...]
    vones[:, :, HD:] = jnp.ones((2, PRE, HD), BF16)

    for load in loads[3:7]:
        load.wait()
    qf[...] = q[...].astype(F32)
    nkf[...] = nk[...].astype(F32)
    nvf[...] = nv[...].astype(F32)
    kloc[LKEYS:] = jnp.zeros((HD, HD), BF16)
    vloc[LKEYS:, :HD] = jnp.zeros((HD, HD), BF16)
    vloc[:, HD:] = jnp.ones((LKEYS + HD, HD), BF16)
    own_i = lax.broadcasted_iota(I32, (BLOCK, LKEYS), 0)
    own_k = lax.broadcasted_iota(I32, (BLOCK, LKEYS), 1)
    own_hit = lax.shift_right_logical(own_k, 6) == own_i
    own_j = lax.bitwise_and(own_k, SUF - 1)
    new_s = lax.broadcasted_iota(I32, (STEPS, BLOCK, HD), 0)
    new_i = lax.broadcasted_iota(I32, (STEPS, BLOCK, HD), 1)
    new_k = lax.broadcasted_iota(I32, (STEPS, BLOCK, HD), 2)
    new_hit = (lax.bitwise_and(new_k, BLOCK - 1) == new_i) & (
        lax.shift_right_logical(new_k, 3) <= new_s
    )

    def local_block(b, carry):
        rows = pl.ds(pl.multiple_of(b * BLOCK, BLOCK), BLOCK)
        query = jnp.concatenate(
            [qf[s, rows, h * HD:(h + 1) * HD] for s in range(STEPS) for h in range(HL)], axis=0
        ).astype(BF16)
        kloc[:LKEYS] = sk[rows].reshape(LKEYS, HD)
        vloc[:LKEYS, :HD] = sv[rows].reshape(LKEYS, HD)
        kloc[LKEYS:LKEYS + STEPS * BLOCK] = nkf[:, rows, :].reshape(STEPS * BLOCK, HD).astype(BF16)
        vloc[LKEYS:LKEYS + STEPS * BLOCK, :HD] = (
            nvf[:, rows, :].reshape(STEPS * BLOCK, HD).astype(BF16)
        )
        length = len_col[rows, :]
        past = dot_t(query, kloc[:LKEYS]).reshape(STEPS * HL, BLOCK, LKEYS)
        past = jnp.where((own_hit & (own_j < length))[None], past, -jnp.inf)
        fresh = dot_t(query, kloc[LKEYS:]).reshape(STEPS, HL, BLOCK, HD)
        fresh = jnp.where(new_hit[:, None], fresh, -jnp.inf)
        past = past.reshape(STEPS * HL * BLOCK, LKEYS)
        fresh = fresh.reshape(STEPS * HL * BLOCK, HD)
        top = jnp.maximum(
            jnp.max(past, axis=-1, keepdims=True), jnp.max(fresh, axis=-1, keepdims=True)
        )
        past = jnp.exp2((past - top) * (SCALE * LOG2E)).astype(BF16)
        fresh = jnp.exp2((fresh - top) * (SCALE * LOG2E)).astype(BF16)
        both = dot(past, vloc[:LKEYS]) + dot(fresh, vloc[LKEYS:])
        total = both[:, HD:]
        shape = (STEPS, HL, BLOCK, HD)
        loc_out[:, :, rows, :] = (both[:, :HD] / total).reshape(shape)
        loc_log[:, :, rows, :] = (top * SCALE + jnp.log(total)).reshape(shape)
        return carry

    lax.fori_loop(0, REQ // BLOCK, local_block, 0)

    lane = lax.broadcasted_iota(I32, (1, 2 * HL, HD), 2)
    place = lax.broadcasted_iota(I32, (1, 2 * HL, HD), 1)
    PART = 16

    def attend(s):
        await_all(q_recv.at[s, pl.ds(1, NW - 1)], qr.at[s])

        def part(i, carry):
            some = pl.ds(i * PART, PART)
            logs = jnp.zeros((PART, 2 * HL, HD), F32)
            for p in range(2):
                query = q_recv[s, some, :, p * HD:(p + 1) * HD].reshape(PART * 2 * HL, HD)
                scores = dot_t(query, pk[p])
                top = jnp.max(scores, axis=-1, keepdims=True)
                weights = jnp.exp2((scores - top) * (SCALE * LOG2E)).astype(BF16)
                both = dot(weights, vones[p])
                total = both[:, HD:]
                result = (both[:, :HD] / total).astype(BF16)
                r_send[s, some, :, p * HD:(p + 1) * HD] = result.reshape(PART, 2 * HL, HD)
                log = (top * SCALE + jnp.log(total)).reshape(PART, 2 * HL, HD)
                logs = jnp.where(lane == place + p * 2 * HL, log, logs)
            l_send[s, some] = jnp.sum(logs, axis=1, keepdims=True)
            return carry

        lax.fori_loop(0, NW // PART, part, 0)
        r_recv[s, 0] = r_send[s, 0]
        l_recv[s, 0] = l_send[s, 0]
        send_results(s)

    own = jnp.broadcast_to(o_col[:REQ], (REQ, HD))
    pick = p_col[:REQ] * (2 * HL) + k_col[:REQ]
    lanes = lax.broadcasted_iota(I32, (REQ, HD), 1)

    def merge(s):
        await_all(r_recv.at[s, pl.ds(1, NW - 1)], rr.at[s])
        await_all(l_recv.at[s, pl.ds(1, NW - 1)], lr.at[s])
        back = dot(gather[0], r_recv[s, :, :, :HD].reshape(ROWS, HD)) + dot(
            gather[1], r_recv[s, :, :, HD:].reshape(ROWS, HD)
        )
        logs = jnp.zeros((REQ, HD), F32)
        for o in range(NW):
            logs = jnp.where(own == o, l_recv[s, o], logs)
        for h in range(HL):
            pre = jnp.sum(jnp.where(lanes == pick + 2 * h, logs, 0.0), axis=1, keepdims=True)
            loc = loc_log[s, h]
            high = jnp.maximum(pre, loc)
            a, b = jnp.exp(pre - high), jnp.exp(loc - high)
            joint = (a * back[h * REQ:(h + 1) * REQ] + b * loc_out[s, h]) / (a + b)
            attn[s, :, h * HD:(h + 1) * HD] = joint.astype(BF16)
        for dest in range(NY):
            for core in range(2):
                n = (dest * 2 + core) * SHARE
                proj[s, core, dest] = dot(attn[s], w[:, n:n + SHARE]).astype(BF16)
        pltpu.make_async_remote_copy(
            src_ref=proj.at[s, 1 - c], dst_ref=c_recv.at[s], send_sem=cs.at[s],
            recv_sem=cr.at[s], device_id=other, device_id_type=MESH,
        ).start()

    def pair(s):
        await_all(c_recv.at[s], cr.at[s])
        y_send[s] = (proj[s, c].astype(F32) + c_recv[s].astype(F32)).astype(BF16)
        for dy in range(1, NY):
            pltpu.make_async_remote_copy(
                src_ref=y_send.at[s, lax.rem(y + dy, NY)], dst_ref=y_recv.at[s, dy - 1],
                send_sem=ys.at[s], recv_sem=yr.at[s], device_id=across(dy), device_id_type=MESH,
            ).start()

    def finish(s):
        await_all(y_recv.at[s], yr.at[s])
        total = y_send[s, y].astype(F32)
        for dy in range(NY - 1):
            total = total + y_recv[s, dy].astype(F32)
        out_v[s] = total.astype(BF16)
        pltpu.make_async_copy(out_v.at[s], out_hbm.at[s], out_sems.at[s]).start()

    attend(0)
    send_queries(2)
    attend(1)
    send_queries(3)
    loads[7].wait()
    merge(0)
    pair(0)
    attend(2)
    merge(1)
    pair(1)
    finish(0)
    attend(3)
    merge(2)
    pair(2)
    finish(1)
    merge(3)
    pair(3)
    finish(2)
    finish(3)

    for s in range(STEPS):
        await_all(q_send.at[s, pl.ds(1, NW - 1)], qs.at[s])
        await_all(r_send.at[s, pl.ds(1, NW - 1)], rs.at[s])
        await_all(l_send.at[s, pl.ds(1, NW - 1)], ls.at[s])
        await_all(c_recv.at[s], cs.at[s])
        await_all(y_recv.at[s], ys.at[s])
        pltpu.make_async_copy(out_v.at[s], out_hbm.at[s], out_sems.at[s]).wait()


def body(
    queries, new_keys, new_values, suffix_keys, suffix_values, suffix_len,
    prefix_keys, prefix_values, prefix_of, out_weight,
):
    anywhere = pl.BlockSpec(memory_space=pl.ANY)
    vmem = pl.BlockSpec(memory_space=pltpu.VMEM)
    pof = prefix_of[:, 0]
    tiled = jnp.tile(pof, HL)
    dma = pltpu.SemaphoreType.DMA
    slots = (STEPS, NW, 2 * HL, 2 * HD)
    logs = (STEPS, NW, 1, HD)
    return pl.pallas_call(
        kernel,
        out_shape=jax.ShapeDtypeStruct((STEPS, REQ, SHARE), BF16),
        in_specs=[anywhere, vmem, vmem, vmem] + [anywhere] * 7,
        out_specs=anywhere,
        scratch_shapes=[
            pltpu.VMEM(queries.shape, BF16),
            pltpu.VMEM(new_keys.shape, BF16),
            pltpu.VMEM(new_values.shape, BF16),
            pltpu.VMEM(suffix_keys.shape, BF16),
            pltpu.VMEM(suffix_values.shape, BF16),
            pltpu.VMEM(prefix_keys.shape, BF16),
            pltpu.VMEM(prefix_values.shape, BF16),
            pltpu.VMEM(out_weight.shape, BF16),
            pltpu.VMEM((2, PRE, 2 * HD), BF16),
            pltpu.VMEM(queries.shape, F32),
            pltpu.VMEM(new_keys.shape, F32),
            pltpu.VMEM(new_values.shape, F32),
            pltpu.VMEM((LKEYS + HD, HD), BF16),
            pltpu.VMEM((LKEYS + HD, 2 * HD), BF16),
            pltpu.VMEM((2, ROWS, ROWS), BF16),
            pltpu.VMEM((2, ROWS, ROWS), BF16),
            pltpu.VMEM(slots, BF16),
            pltpu.VMEM(slots, BF16),
            pltpu.VMEM(slots, BF16),
            pltpu.VMEM(slots, BF16),
            pltpu.VMEM(logs, F32),
            pltpu.VMEM(logs, F32),
            pltpu.VMEM((STEPS, HL, REQ, HD), F32),
            pltpu.VMEM((STEPS, HL, REQ, HD), F32),
            pltpu.VMEM((STEPS, REQ, HL * HD), BF16),
            pltpu.VMEM((STEPS, 2, NY, REQ, SHARE), BF16),
            pltpu.VMEM((STEPS, NY, REQ, SHARE), BF16),
            pltpu.VMEM((STEPS, NY, REQ, SHARE), BF16),
            pltpu.VMEM((STEPS, NY - 1, REQ, SHARE), BF16),
            pltpu.VMEM((STEPS, REQ, SHARE), BF16),
            dma((8,)),
            dma((STEPS,)),
        ] + [dma((STEPS,))] * 10,
        compiler_params=pltpu.CompilerParams(
            collective_id=0, has_side_effects=True, vmem_limit_bytes=48 * 2**20
        ),
        name="attention",
    )(
        queries, tiled[None, :], tiled[:, None], suffix_len[:, None], new_keys, new_values,
        suffix_keys, suffix_values, prefix_keys, prefix_values, out_weight,
    )


def solution(mesh):
    return jax.shard_map(
        body,
        mesh=mesh,
        in_specs=(
            P(None, "wide", "tensor"),
            P(None, "wide", "tensor"),
            P(None, "wide", "tensor"),
            P("wide", None, "tensor"),
            P("wide", None, "tensor"),
            P("wide"),
            P("wide", None, "tensor"),
            P("wide", None, "tensor"),
            P("wide", None),
            P("tensor", None),
        ),
        out_specs=P(None, "wide", "tensor"),
        check_vma=False,
    )
```

time: 327 us -> 81.4 us (0.25)
  waiting for transfers between devices: 155 us -> 0 us
  Pallas kernels: 0 us -> 71.4 us
  starting transfers between devices: 68.3 us -> 0 us
  matrix products: 29.8 us -> 0 us
  local copies, waits for them, and re-layouts: 34 us -> 9.53 us
  other arithmetic: 23.5 us -> 0 us
  between operations: 13.9 us -> 0.03 us
    psum x1 -> x0, waiting for transfers between devices: 79.5 us -> none  [body(): lax.psum(head_terms.astype(jnp.bfloat16), 'tensor').astype(jnp.float32)]
    all_to_all x12 -> x0, waiting for transfers between devices: 75 us -> none  [the longest x4 31.8 us: body(): lax.all_to_all(outgoing[:, :, step_index:step_index + 1], 'wide', split_a...]
    pallas_call x0 -> x1, Pallas kernels: none -> 71.4 us  [body(): pl.pallas_call(kernel, out_shape=jax.ShapeDtypeStruct((STEPS, REQ, SHARE)...]
    all_to_all x12 -> x0, starting transfers between devices: 68.1 us -> none  [the longest x4 25.1 us: body(): lax.all_to_all(outgoing[:, :, step_index:step_index + 1], 'wide', split_a...]
    dot_general x11 -> x0, matrix products: 29.8 us -> none  [the longest x4 10.2 us: owner_attend(): jnp.einsum('pgqk,pkgd->pgqd', weights.astype(jnp.bfloat16), head_values,...]
    reduce_sum x6 -> x0, other arithmetic: 9.6 us -> none  [the longest x4 7.99 us: owner_attend(): totals = jnp.sum(weights, axis=-1, keepdims=True)]
    reshape x18 -> x0, local copies, waits for them, and re-layouts: 7.62 us -> none  [the longest x4 3.46 us: owner_attend(): (numerator / totals).reshape(owned_count, kv_heads, sources, capacity, st...]
    add x5 -> x0, local copies, waits for them, and re-layouts: 6.63 us -> none  [the longest x4 5.88 us: owner_attend(): highest[..., 0] + jnp.log(totals[..., 0])]
  transfers between devices with their start and end apart: 13 -> 0, of which waited for: 12 -> 0; matrix products, arithmetic and copies ran while one was open for 16% -> 0% of each run, Pallas kernels for 0% -> 0%
where the time goes in v1:
time: 81.4 us; the launch traced here: 81 us
  Pallas kernels  71.4 us (88%)
  local copies, waits for them, and re-layouts  9.53 us (12%)
    pallas_call x1, Pallas kernels, body(): pl.pallas_call(kernel, out_shape=jax.ShapeDtypeStruct((STEPS, REQ, SHARE)...  71.4 us
    unnamed x15, local copies, waits for them, and re-layouts  7.86 us

profile of v1, /device:TPU:1, one launch (start us, length us, event | category | flops | bytes accessed | tf_op | source)
XLA Modules:
  0.0 81.0 jit_solution(6520540404717400704)
XLA Ops:
  0.0 0.7 tile.8
  0.7 0.1 broadcast_in_dim_tile.6.pof_row
  0.7 0.7 copy.13.len_col
  1.5 0.2 broadcast_in_dim_tile.8.pof_col
  1.7 0.0 copy-start
  1.7 1.2 %copy-done = bf16[64,64,128]{2,1,0:T(8,128)(2,1)S(1)} copy-done((bf16[64,64,128]{2,1,0:T(8,128)(2,1)S(1)}, bf16[64,64,128]{2,1,0:T(8,128)(2,1)}, u32[]{:S(2)}) %copy-start) | copy-done | bytes 1048600
  2.9 0.0 copy-start.1
  2.9 1.2 %copy-done.1 = bf16[64,64,128]{2,1,0:T(8,128)(2,1)S(1)} copy-done((bf16[64,64,128]{2,1,0:T(8,128)(2,1)S(1)}, bf16[64,64,128]{2,1,0:T(8,128)(2,1)}, u32[]{:S(2)}) %copy-start.1) | copy-done | bytes 1048600
  4.1 0.0 copy-start.2
  4.1 1.0 %copy-done.2 = bf16[4,64,1024]{2,1,0:T(8,128)(2,1)S(1)} copy-done((bf16[4,64,1024]{2,1,0:T(8,128)(2,1)S(1)}, bf16[4,64,1024]{2,1,0:T(8,128)(2,1)}, u32[]{:S(2)}) %copy-start.2) | copy-done | bytes 524312
  5.2 0.0 copy-start.3
  5.2 1.0 %copy-done.3 = bf16[2,768,128]{2,1,0:T(8,128)(2,1)S(1)} copy-done((bf16[2,768,128]{2,1,0:T(8,128)(2,1)S(1)}, bf16[2,768,128]{2,1,0:T(8,128)(2,1)}, u32[]{:S(2)}) %copy-start.3) | copy-done | bytes 393240
  6.2 0.0 copy-start.4
  6.2 1.0 %copy-done.4 = bf16[2,768,128]{2,1,0:T(8,128)(2,1)S(1)} copy-done((bf16[2,768,128]{2,1,0:T(8,128)(2,1)S(1)}, bf16[2,768,128]{2,1,0:T(8,128)(2,1)}, u32[]{:S(2)}) %copy-start.4) | copy-done | bytes 393240
  7.2 0.0 copy-start.5
  7.2 0.8 %copy-done.5 = bf16[4,64,128]{2,1,0:T(8,128)(2,1)S(1)} copy-done((bf16[4,64,128]{2,1,0:T(8,128)(2,1)S(1)}, bf16[4,64,128]{2,1,0:T(8,128)(2,1)}, u32[]{:S(2)}) %copy-start.5) | copy-done | bytes 65560
  8.0 0.0 copy-start.6
  8.0 0.8 %copy-done.6 = bf16[4,64,128]{2,1,0:T(8,128)(2,1)S(1)} copy-done((bf16[4,64,128]{2,1,0:T(8,128)(2,1)S(1)}, bf16[4,64,128]{2,1,0:T(8,128)(2,1)}, u32[]{:S(2)}) %copy-start.6) | copy-done | bytes 65560
  8.9 71.4 %attention.1 = bf16[4,64,512]{2,1,0:T(8,128)(2,1)S(1)} custom-call(bf16[4,64,1024]{2,1,0:T(8,128)(2,1)S(1)} %copy-done.2, s32[1,512]{1,0:T(1,128)S(1)} %broadcast_in_dim_tile.6.pof_row, s32[512,1]{1,0:T(8,128)S(1)} %broadcast_in_dim_tile.8.pof_col, s32[64,1]{1,0:T(8,128)S(1)} %copy.13.len_col, bf16[4,64,128]{2,1,0:T(8,128)(2,1)S(1)} %copy-done.5, ...), custom_call_target="tpu_custom_call" | custom-call | tf_op jit(solution)/shard_map/attention/pallas_call | solution.py:336
  80.3 0.7 copy.15
Async XLA Ops:
  1.7 1.2 %copy-start = (bf16[64,64,128]{2,1,0:T(8,128)(2,1)S(1)}, bf16[64,64,128]{2,1,0:T(8,128)(2,1)}, u32[]{:S(2)}) copy-start(bf16[64,64,128]{2,1,0:T(8,128)(2,1)} %sk_hbm.1) | copy-start | bytes 3145732
  2.9 1.2 %copy-start.1 = (bf16[64,64,128]{2,1,0:T(8,128)(2,1)S(1)}, bf16[64,64,128]{2,1,0:T(8,128)(2,1)}, u32[]{:S(2)}) copy-start(bf16[64,64,128]{2,1,0:T(8,128)(2,1)} %sv_hbm.1) | copy-start | bytes 3145732
  4.1 1.0 %copy-start.2 = (bf16[4,64,1024]{2,1,0:T(8,128)(2,1)S(1)}, bf16[4,64,1024]{2,1,0:T(8,128)(2,1)}, u32[]{:S(2)}) copy-start(bf16[4,64,1024]{2,1,0:T(8,128)(2,1)} %q_hbm.1) | copy-start | bytes 1572868
  5.2 1.0 %copy-start.3 = (bf16[2,768,128]{2,1,0:T(8,128)(2,1)S(1)}, bf16[2,768,128]{2,1,0:T(8,128)(2,1)}, u32[]{:S(2)}) copy-start(bf16[2,768,128]{2,1,0:T(8,128)(2,1)} %pk_hbm.1) | copy-start | bytes 1179652
  6.2 1.0 %copy-start.4 = (bf16[2,768,128]{2,1,0:T(8,128)(2,1)S(1)}, bf16[2,768,128]{2,1,0:T(8,128)(2,1)}, u32[]{:S(2)}) copy-start(bf16[2,768,128]{2,1,0:T(8,128)(2,1)} %pv_hbm.1) | copy-start | bytes 1179652
  7.2 0.8 %copy-start.5 = (bf16[4,64,128]{2,1,0:T(8,128)(2,1)S(1)}, bf16[4,64,128]{2,1,0:T(8,128)(2,1)}, u32[]{:S(2)}) copy-start(bf16[4,64,128]{2,1,0:T(8,128)(2,1)} %nk_hbm.1) | copy-start | bytes 196612
  8.0 0.8 %copy-start.6 = (bf16[4,64,128]{2,1,0:T(8,128)(2,1)S(1)}, bf16[4,64,128]{2,1,0:T(8,128)(2,1)}, u32[]{:S(2)}) copy-start(bf16[4,64,128]{2,1,0:T(8,128)(2,1)} %nv_hbm.1) | copy-start | bytes 196612

commit v2 on v1

--- a/solution.py
+++ b/solution.py
@@ -32,11 +32,12 @@
 
 
 def kernel(
-    q_hbm, pof_row, pof_col, len_col, nk_hbm, nv_hbm, sk_hbm, sv_hbm, pk_hbm, pv_hbm, w_hbm,
+    q_hbm, pof_ref, len_ref, nk_hbm, nv_hbm, sk_hbm, sv_hbm, pk_hbm, pv_hbm, w_hbm,
     out_hbm,
     q, nk, nv, sk, sv, pk, pv, w, vones, qf, nkf, nvf, kloc, vloc,
+    len_col,
     spread, gather, q_send, q_recv, r_send, r_recv, l_send, l_recv,
-    loc_out, loc_log, attn, proj, c_recv, y_send, y_recv, out_v,
+    loc_out, loc_log, pre_part, attn, kept, given, c_recv, y_send, y_recv, out_v,
     in_sems, out_sems, qs, qr, rs, rr, ls, lr, cs, cr, ys, yr,
 ):
     me_w, me_t = lax.axis_index("wide"), lax.axis_index("tensor")
@@ -64,7 +65,8 @@
         pltpu.make_async_copy(src, dst, in_sems.at[n])
         for n, (src, dst) in enumerate(
             [(q_hbm, q), (pk_hbm, pk), (pv_hbm, pv), (nk_hbm, nk), (nv_hbm, nv),
-             (sk_hbm, sk), (sv_hbm, sv), (w_hbm, w)]
+             (sk_hbm, sk), (sv_hbm, sv)]
+            + [(w_hbm.at[:, pl.ds(n * SHARE, SHARE)], w.at[n]) for n in range(2 * NY)]
         )
     ]
     for load in loads:
@@ -81,25 +83,30 @@
         pl.semaphore_signal(barrier, inc=1, device_id=across(dy), device_id_type=MESH)
     pl.semaphore_signal(barrier, inc=1, device_id=other, device_id_type=MESH)
 
-    def slot_of(pof, rank):
-        owner = lax.shift_right_logical(pof, 1)
-        dz = lax.bitwise_and(lax.shift_right_logical(owner, 2) - z + NZ, NZ - 1)
-        dx = lax.bitwise_and(lax.bitwise_and(owner, NX - 1) - x + NX, NX - 1)
-        return dz * NX + dx, lax.bitwise_and(pof, 1), rank
-
-    prow = pof_row[...]
-    pcol = pof_col[...]
-    same = pcol[:REQ] == prow
-    before = lax.broadcasted_iota(I32, (REQ, ROWS), 0) < lax.bitwise_and(
-        lax.broadcasted_iota(I32, (REQ, ROWS), 1), REQ - 1
+    pof = pof_ref[...]
+    sub = lax.broadcasted_iota(I32, (REQ, REQ), 0)
+    lane = lax.broadcasted_iota(I32, (REQ, REQ), 1)
+
+    def upright(row):
+        return jnp.sum(jnp.where(sub == lane, row, 0), axis=1, keepdims=True)
+
+    rank = jnp.sum(
+        jnp.where((upright(pof) == pof) & (sub < lane), 1, 0), axis=0, keepdims=True
     )
-    rank_row = jnp.sum(jnp.where(same & before, 1, 0), axis=0, keepdims=True)
-    o_row, p_row, k_row = slot_of(prow, rank_row)
-    head_row = lax.shift_right_logical(lax.broadcasted_iota(I32, (1, ROWS), 1), 6)
-    key_row = (o_row * HL + head_row) * 2 + k_row
+    owner = lax.shift_right_logical(pof, 1)
+    dz = lax.bitwise_and(lax.shift_right_logical(owner, 2) - z + NZ, NZ - 1)
+    dx = lax.bitwise_and(lax.bitwise_and(owner, NX - 1) - x + NX, NX - 1)
+    slot = (lax.bitwise_and(pof, 1) * NW + dz * NX + dx) * (2 * HL) + rank
+    slot_col = upright(slot)
+    wide_sub = lax.broadcasted_iota(I32, (REQ, ROWS), 0)
+    wide_lane = lax.broadcasted_iota(I32, (REQ, ROWS), 1)
+    key_row = jnp.sum(
+        jnp.where(wide_sub == lax.bitwise_and(wide_lane, REQ - 1), slot_col, 0),
+        axis=0, keepdims=True,
+    ) + 2 * lax.shift_right_logical(lax.broadcasted_iota(I32, (1, ROWS), 1), 6)
     slot_rows = lax.broadcasted_iota(I32, (ROWS, ROWS), 0)
     for p in range(2):
-        hit = slot_rows == jnp.where(p_row == p, key_row, -1)
+        hit = slot_rows == key_row - p * ROWS
         spread[p] = jnp.where(hit, 1.0, 0.0).astype(BF16)
 
     loads[0].wait()
@@ -131,6 +138,14 @@
                 src_ref=r_send.at[s, o], dst_ref=r_recv.at[s, o], send_sem=rs.at[s],
                 recv_sem=rr.at[s], device_id=behind(dz, dx), device_id_type=MESH,
             ).start()
+            return carry
+
+        lax.fori_loop(1, NW, one, 0)
+
+    def send_logs(s):
+        def one(i, carry):
+            dz, dx = offset(NW - i)
+            o = dz * NX + dx
             pltpu.make_async_remote_copy(
                 src_ref=l_send.at[s, o], dst_ref=l_recv.at[s, o], send_sem=ls.at[s],
                 recv_sem=lr.at[s], device_id=behind(dz, dx), device_id_type=MESH,
@@ -150,18 +165,17 @@
     dispatch(2)
     dispatch(3)
 
-    same_c = pcol == prow[:, :REQ]
-    before_c = lax.broadcasted_iota(I32, (ROWS, REQ), 1) < lax.bitwise_and(
-        lax.broadcasted_iota(I32, (ROWS, REQ), 0), REQ - 1
-    )
-    rank_col = jnp.sum(jnp.where(same_c & before_c, 1, 0), axis=1, keepdims=True)
-    o_col, p_col, k_col = slot_of(pcol, rank_col)
-    head_col = lax.shift_right_logical(lax.broadcasted_iota(I32, (ROWS, 1), 0), 6)
-    key_col = (o_col * HL + head_col) * 2 + k_col
+    tall_sub = lax.broadcasted_iota(I32, (ROWS, REQ), 0)
+    tall_lane = lax.broadcasted_iota(I32, (ROWS, REQ), 1)
+    key_col = jnp.sum(
+        jnp.where(lax.bitwise_and(tall_sub, REQ - 1) == tall_lane, slot, 0),
+        axis=1, keepdims=True,
+    ) + 2 * lax.shift_right_logical(lax.broadcasted_iota(I32, (ROWS, 1), 0), 6)
     slot_cols = lax.broadcasted_iota(I32, (ROWS, ROWS), 1)
     for p in range(2):
-        hit = slot_cols == jnp.where(p_col == p, key_col, -1)
+        hit = slot_cols == key_col - p * ROWS
         gather[p] = jnp.where(hit, 1.0, 0.0).astype(BF16)
+    len_col[...] = jnp.broadcast_to(upright(len_ref[...]), (REQ, HD))
     loads[1].wait()
     loads[2].wait()
     vones[:, :, :HD] = pv[...]
@@ -197,7 +211,7 @@
         vloc[LKEYS:LKEYS + STEPS * BLOCK, :HD] = (
             nvf[:, rows, :].reshape(STEPS * BLOCK, HD).astype(BF16)
         )
-        length = len_col[rows, :]
+        length = len_col[rows, :1]
         past = dot_t(query, kloc[:LKEYS]).reshape(STEPS * HL, BLOCK, LKEYS)
         past = jnp.where((own_hit & (own_j < length))[None], past, -jnp.inf)
         fresh = dot_t(query, kloc[LKEYS:]).reshape(STEPS, HL, BLOCK, HD)
@@ -218,7 +232,7 @@
 
     lax.fori_loop(0, REQ // BLOCK, local_block, 0)
 
-    lane = lax.broadcasted_iota(I32, (1, 2 * HL, HD), 2)
+    log_lane = lax.broadcasted_iota(I32, (1, 2 * HL, HD), 2)
     place = lax.broadcasted_iota(I32, (1, 2 * HL, HD), 1)
     PART = 16
 
@@ -238,25 +252,24 @@
                 result = (both[:, :HD] / total).astype(BF16)
                 r_send[s, some, :, p * HD:(p + 1) * HD] = result.reshape(PART, 2 * HL, HD)
                 log = (top * SCALE + jnp.log(total)).reshape(PART, 2 * HL, HD)
-                logs = jnp.where(lane == place + p * 2 * HL, log, logs)
+                logs = jnp.where(log_lane == place + p * 2 * HL, log, logs)
             l_send[s, some] = jnp.sum(logs, axis=1, keepdims=True)
             return carry
 
         lax.fori_loop(0, NW // PART, part, 0)
         r_recv[s, 0] = r_send[s, 0]
         l_recv[s, 0] = l_send[s, 0]
+        send_logs(s)
         send_results(s)
 
-    own = jnp.broadcast_to(o_col[:REQ], (REQ, HD))
-    pick = p_col[:REQ] * (2 * HL) + k_col[:REQ]
+    own = jnp.broadcast_to(
+        lax.bitwise_and(lax.shift_right_logical(slot_col, 4), NW - 1), (REQ, HD)
+    )
+    pick = lax.shift_right_logical(slot_col, 9) * (2 * HL) + lax.bitwise_and(slot_col, 1)
     lanes = lax.broadcasted_iota(I32, (REQ, HD), 1)
 
     def merge(s):
-        await_all(r_recv.at[s, pl.ds(1, NW - 1)], rr.at[s])
         await_all(l_recv.at[s, pl.ds(1, NW - 1)], lr.at[s])
-        back = dot(gather[0], r_recv[s, :, :, :HD].reshape(ROWS, HD)) + dot(
-            gather[1], r_recv[s, :, :, HD:].reshape(ROWS, HD)
-        )
         logs = jnp.zeros((REQ, HD), F32)
         for o in range(NW):
             logs = jnp.where(own == o, l_recv[s, o], logs)
@@ -265,29 +278,58 @@
             loc = loc_log[s, h]
             high = jnp.maximum(pre, loc)
             a, b = jnp.exp(pre - high), jnp.exp(loc - high)
-            joint = (a * back[h * REQ:(h + 1) * REQ] + b * loc_out[s, h]) / (a + b)
+            pre_part[h] = a / (a + b)
+            loc_out[s, h] = loc_out[s, h] * (b / (a + b))
+        await_all(r_recv.at[s, pl.ds(1, NW - 1)], rr.at[s])
+        back = dot(gather[0], r_recv[s, :, :, :HD].reshape(ROWS, HD)) + dot(
+            gather[1], r_recv[s, :, :, HD:].reshape(ROWS, HD)
+        )
+        for h in range(HL):
+            joint = pre_part[h] * back[h * REQ:(h + 1) * REQ] + loc_out[s, h]
             attn[s, :, h * HD:(h + 1) * HD] = joint.astype(BF16)
-        for dest in range(NY):
-            for core in range(2):
-                n = (dest * 2 + core) * SHARE
-                proj[s, core, dest] = dot(attn[s], w[:, n:n + SHARE]).astype(BF16)
+
+    def block(dy, core):
+        return lax.rem(y + dy, NY) * 2 + core
+
+    def give(s, dy):
+        given[s, dy] = dot(attn[s], w[block(dy, 1 - c)]).astype(BF16)
         pltpu.make_async_remote_copy(
-            src_ref=proj.at[s, 1 - c], dst_ref=c_recv.at[s], send_sem=cs.at[s],
-            recv_sem=cr.at[s], device_id=other, device_id_type=MESH,
+            src_ref=given.at[s, dy], dst_ref=c_recv.at[s, dy], send_sem=cs.at[s, dy],
+            recv_sem=cr.at[s, dy], device_id=other, device_id_type=MESH,
         ).start()
 
-    def pair(s):
-        await_all(c_recv.at[s], cr.at[s])
-        y_send[s] = (proj[s, c].astype(F32) + c_recv[s].astype(F32)).astype(BF16)
-        for dy in range(1, NY):
-            pltpu.make_async_remote_copy(
-                src_ref=y_send.at[s, lax.rem(y + dy, NY)], dst_ref=y_recv.at[s, dy - 1],
-                send_sem=ys.at[s], recv_sem=yr.at[s], device_id=across(dy), device_id_type=MESH,
-            ).start()
+    def keep(s, dy):
+        kept[s, dy] = dot(attn[s], w[block(dy, c)])
+
+    def pair(s, dy):
+        await_all(c_recv.at[s, dy], cr.at[s, dy])
+        both = kept[s, dy] + c_recv[s, dy].astype(F32)
+        if dy == 0:
+            kept[s, dy] = both
+            return
+        y_send[s, dy - 1] = both.astype(BF16)
+        pltpu.make_async_remote_copy(
+            src_ref=y_send.at[s, dy - 1], dst_ref=y_recv.at[s, dy - 1],
+            send_sem=ys.at[s], recv_sem=yr.at[s], device_id=across(dy), device_id_type=MESH,
+        ).start()
+
+    def project(s):
+        give(s, 2)
+        give(s, 1)
+        give(s, 3)
+        keep(s, 2)
+        keep(s, 1)
+        pair(s, 2)
+        keep(s, 3)
+        pair(s, 1)
+        give(s, 0)
+        pair(s, 3)
+        keep(s, 0)
+        pair(s, 0)
 
     def finish(s):
         await_all(y_recv.at[s], yr.at[s])
-        total = y_send[s, y].astype(F32)
+        total = kept[s, 0]
         for dy in range(NY - 1):
             total = total + y_recv[s, dy].astype(F32)
         out_v[s] = total.astype(BF16)
@@ -297,19 +339,20 @@
     send_queries(2)
     attend(1)
     send_queries(3)
-    loads[7].wait()
+    for load in loads[7:]:
+        load.wait()
     merge(0)
-    pair(0)
+    project(0)
     attend(2)
     merge(1)
-    pair(1)
+    project(1)
     finish(0)
     attend(3)
     merge(2)
-    pair(2)
+    project(2)
     finish(1)
     merge(3)
-    pair(3)
+    project(3)
     finish(2)
     finish(3)
 
@@ -317,8 +360,9 @@
         await_all(q_send.at[s, pl.ds(1, NW - 1)], qs.at[s])
         await_all(r_send.at[s, pl.ds(1, NW - 1)], rs.at[s])
         await_all(l_send.at[s, pl.ds(1, NW - 1)], ls.at[s])
-        await_all(c_recv.at[s], cs.at[s])
-        await_all(y_recv.at[s], ys.at[s])
+        for dy in range(NY):
+            await_all(given.at[s, dy], cs.at[s, dy])
+        await_all(y_send.at[s], ys.at[s])
         pltpu.make_async_copy(out_v.at[s], out_hbm.at[s], out_sems.at[s]).wait()
 
 
@@ -328,15 +372,13 @@
 ):
     anywhere = pl.BlockSpec(memory_space=pl.ANY)
     vmem = pl.BlockSpec(memory_space=pltpu.VMEM)
-    pof = prefix_of[:, 0]
-    tiled = jnp.tile(pof, HL)
     dma = pltpu.SemaphoreType.DMA
     slots = (STEPS, NW, 2 * HL, 2 * HD)
     logs = (STEPS, NW, 1, HD)
     return pl.pallas_call(
         kernel,
         out_shape=jax.ShapeDtypeStruct((STEPS, REQ, SHARE), BF16),
-        in_specs=[anywhere, vmem, vmem, vmem] + [anywhere] * 7,
+        in_specs=[anywhere, vmem, vmem] + [anywhere] * 7,
         out_specs=anywhere,
         scratch_shapes=[
             pltpu.VMEM(queries.shape, BF16),
@@ -346,13 +388,14 @@
             pltpu.VMEM(suffix_values.shape, BF16),
             pltpu.VMEM(prefix_keys.shape, BF16),
             pltpu.VMEM(prefix_values.shape, BF16),
-            pltpu.VMEM(out_weight.shape, BF16),
+            pltpu.VMEM((2 * NY, out_weight.shape[0], SHARE), BF16),
             pltpu.VMEM((2, PRE, 2 * HD), BF16),
             pltpu.VMEM(queries.shape, F32),
             pltpu.VMEM(new_keys.shape, F32),
             pltpu.VMEM(new_values.shape, F32),
             pltpu.VMEM((LKEYS + HD, HD), BF16),
             pltpu.VMEM((LKEYS + HD, 2 * HD), BF16),
+            pltpu.VMEM((REQ, HD), I32),
             pltpu.VMEM((2, ROWS, ROWS), BF16),
             pltpu.VMEM((2, ROWS, ROWS), BF16),
             pltpu.VMEM(slots, BF16),
@@ -363,21 +406,23 @@
             pltpu.VMEM(logs, F32),
             pltpu.VMEM((STEPS, HL, REQ, HD), F32),
             pltpu.VMEM((STEPS, HL, REQ, HD), F32),
+            pltpu.VMEM((HL, REQ, HD), F32),
             pltpu.VMEM((STEPS, REQ, HL * HD), BF16),
-            pltpu.VMEM((STEPS, 2, NY, REQ, SHARE), BF16),
+            pltpu.VMEM((STEPS, NY, REQ, SHARE), F32),
             pltpu.VMEM((STEPS, NY, REQ, SHARE), BF16),
             pltpu.VMEM((STEPS, NY, REQ, SHARE), BF16),
             pltpu.VMEM((STEPS, NY - 1, REQ, SHARE), BF16),
+            pltpu.VMEM((STEPS, NY - 1, REQ, SHARE), BF16),
             pltpu.VMEM((STEPS, REQ, SHARE), BF16),
-            dma((8,)),
+            dma((7 + 2 * NY,)),
             dma((STEPS,)),
-        ] + [dma((STEPS,))] * 10,
+        ] + [dma((STEPS,))] * 6 + [dma((STEPS, NY))] * 2 + [dma((STEPS,))] * 2,
         compiler_params=pltpu.CompilerParams(
-            collective_id=0, has_side_effects=True, vmem_limit_bytes=48 * 2**20
+            collective_id=0, has_side_effects=True, vmem_limit_bytes=62 * 2**20
         ),
         name="attention",
     )(
-        queries, tiled[None, :], tiled[:, None], suffix_len[:, None], new_keys, new_values,
+        queries, prefix_of.reshape(1, REQ), suffix_len.reshape(1, REQ), new_keys, new_values,
         suffix_keys, suffix_values, prefix_keys, prefix_values, out_weight,
     )
 

time: 81.4 us -> 74.3 us (0.913)
  local copies, waits for them, and re-layouts: 9.53 us -> 1.67 us
  Pallas kernels: 71.4 us -> 72.5 us
    unnamed x15 -> x1, local copies, waits for them, and re-layouts: 7.86 us -> 1.67 us
    pallas_call x1, Pallas kernels: 71.4 us -> 72.5 us  [body(): pl.pallas_call(kernel, out_shape=jax.ShapeDtypeStruct((STEPS, REQ, SHARE)...]
    another operation x3 -> x0, local copies, waits for them, and re-layouts: 0.93 us -> none  [the longest x1 0.66 us: body(): tiled = jnp.tile(pof, HL)]
where the time goes in v2:
time: 74.3 us; the launch traced here: 74.2 us
  Pallas kernels  72.5 us (98%)
  local copies, waits for them, and re-layouts  1.67 us (2%)
    pallas_call x1, Pallas kernels, body(): pl.pallas_call(kernel, out_shape=jax.ShapeDtypeStruct((STEPS, REQ, SHARE)...  72.5 us
    unnamed x1, local copies, waits for them, and re-layouts  1.67 us

profile of v2, /device:TPU:1, one launch (start us, length us, event | category | flops | bytes accessed | tf_op | source)
XLA Modules:
  0.0 74.2 jit_solution(7085136365970898319)
XLA Ops:
  0.0 72.5 %attention.1 = bf16[4,64,512]{2,1,0:T(8,128)(2,1)} custom-call(bf16[4,64,1024]{2,1,0:T(8,128)(2,1)} %q_hbm.1, s32[1,64]{1,0:T(1,128)} %bitcast.2, s32[1,64]{1,0:T(1,128)} %bitcast.3, bf16[4,64,128]{2,1,0:T(8,128)(2,1)} %nk_hbm.1, bf16[4,64,128]{2,1,0:T(8,128)(2,1)} %nv_hbm.1, bf16[64,64,128]{2,1,0:T(8,128)(2,1)} %sk_hbm.1, bf16[64,64,128]{2,1,0:T(8,128)(2,1)} %sv_hbm.1, ...), custom_call_target="tpu_custom_call" | custom-call | tf_op jit(solution)/shard_map/attention/pallas_call | solution.py:378
  72.5 1.7 %copy.12 = bf16[4,64,512]{2,1,0:T(8,128)(2,1)} copy(bf16[4,64,512]{2,1,0:T(8,128)(2,1)} %attention.1) | data formatting | bytes 524288

commit v3 on v2

--- a/solution.py
+++ b/solution.py
@@ -14,6 +14,8 @@
 STEPS, REQ, HL = 4, 64, 8
 PRE, SUF = 768, 64
 ROWS = HL * REQ
+HALF = ROWS // 2
+LAST = STEPS - 1
 SCALE = HD ** (-0.5)
 LOG2E = 1.4426950408889634
 BLOCK = 8
@@ -33,11 +35,11 @@
 
 def kernel(
     q_hbm, pof_ref, len_ref, nk_hbm, nv_hbm, sk_hbm, sv_hbm, pk_hbm, pv_hbm, w_hbm,
-    out_hbm,
+    own_hbm, y_recv,
     q, nk, nv, sk, sv, pk, pv, w, vones, qf, nkf, nvf, kloc, vloc,
     len_col,
     spread, gather, q_send, q_recv, r_send, r_recv, l_send, l_recv,
-    loc_out, loc_log, pre_part, attn, kept, given, c_recv, y_send, y_recv, out_v,
+    loc_out, loc_log, pre_part, attn, early, kept, given, c_recv, y_send,
     in_sems, out_sems, qs, qr, rs, rr, ls, lr, cs, cr, ys, yr,
 ):
     me_w, me_t = lax.axis_index("wide"), lax.axis_index("tensor")
@@ -64,12 +66,12 @@
     loads = [
         pltpu.make_async_copy(src, dst, in_sems.at[n])
         for n, (src, dst) in enumerate(
-            [(q_hbm, q), (pk_hbm, pk), (pv_hbm, pv), (nk_hbm, nk), (nv_hbm, nv),
-             (sk_hbm, sk), (sv_hbm, sv)]
+            [(q_hbm.at[s], q.at[s]) for s in range(STEPS)]
+            + [(pk_hbm, pk), (pv_hbm, pv), (nk_hbm, nk), (nv_hbm, nv), (sk_hbm, sk), (sv_hbm, sv)]
             + [(w_hbm.at[:, pl.ds(n * SHARE, SHARE)], w.at[n]) for n in range(2 * NY)]
         )
     ]
-    for load in loads:
+    for load in loads[:STEPS]:
         load.start()
 
     barrier = pltpu.get_barrier_semaphore()
@@ -96,27 +98,26 @@
     owner = lax.shift_right_logical(pof, 1)
     dz = lax.bitwise_and(lax.shift_right_logical(owner, 2) - z + NZ, NZ - 1)
     dx = lax.bitwise_and(lax.bitwise_and(owner, NX - 1) - x + NX, NX - 1)
-    slot = (lax.bitwise_and(pof, 1) * NW + dz * NX + dx) * (2 * HL) + rank
+    slot = (dz * NX + dx) * 16 + lax.bitwise_and(pof, 1) * 8 + rank
     slot_col = upright(slot)
-    wide_sub = lax.broadcasted_iota(I32, (REQ, ROWS), 0)
-    wide_lane = lax.broadcasted_iota(I32, (REQ, ROWS), 1)
+    wide_sub = lax.broadcasted_iota(I32, (REQ, HALF), 0)
+    wide_lane = lax.broadcasted_iota(I32, (REQ, HALF), 1)
     key_row = jnp.sum(
         jnp.where(wide_sub == lax.bitwise_and(wide_lane, REQ - 1), slot_col, 0),
         axis=0, keepdims=True,
-    ) + 2 * lax.shift_right_logical(lax.broadcasted_iota(I32, (1, ROWS), 1), 6)
-    slot_rows = lax.broadcasted_iota(I32, (ROWS, ROWS), 0)
-    for p in range(2):
-        hit = slot_rows == key_row - p * ROWS
-        spread[p] = jnp.where(hit, 1.0, 0.0).astype(BF16)
-
-    loads[0].wait()
+    ) + 2 * lax.shift_right_logical(lax.broadcasted_iota(I32, (1, HALF), 1), 6)
+    hit = lax.broadcasted_iota(I32, (ROWS, HALF), 0) == key_row
+    spread[...] = jnp.where(hit, 1.0, 0.0).astype(BF16)
 
     def dispatch(s):
-        stacked = jnp.concatenate([q[s, :, h * HD:(h + 1) * HD] for h in range(HL)], axis=0)
-        for p in range(2):
-            placed = dot(spread[p], stacked).astype(BF16).reshape(NW, 2 * HL, HD)
-            q_send[s, :, :, p * HD:(p + 1) * HD] = placed
-            q_recv[s, 0, :, p * HD:(p + 1) * HD] = placed[0]
+        loads[s].wait()
+        for half in range(2):
+            stacked = jnp.concatenate(
+                [q[s, :, h * HD:(h + 1) * HD] for h in range(half * 4, half * 4 + 4)], axis=0
+            )
+            placed = dot(spread[...], stacked).astype(BF16).reshape(NW, 16, HD)
+            q_send[s, :, half] = placed
+            q_recv[s, 0, half] = placed[0]
 
     def send_queries(s):
         def one(i, carry):
@@ -130,13 +131,16 @@
 
         lax.fori_loop(1, NW, one, 0)
 
-    def send_results(s):
+    def send_results(s, half=None):
+        part = pl.ds(0, 2) if half is None else pl.ds(half, 1)
+
         def one(i, carry):
             dz, dx = offset(NW - i)
             o = dz * NX + dx
             pltpu.make_async_remote_copy(
-                src_ref=r_send.at[s, o], dst_ref=r_recv.at[s, o], send_sem=rs.at[s],
-                recv_sem=rr.at[s], device_id=behind(dz, dx), device_id_type=MESH,
+                src_ref=r_send.at[s, o, part], dst_ref=r_recv.at[s, o, part],
+                send_sem=rs.at[s + (half or 0)], recv_sem=rr.at[s + (half or 0)],
+                device_id=behind(dz, dx), device_id_type=MESH,
             ).start()
             return carry
 
@@ -160,28 +164,29 @@
     dispatch(0)
     pl.semaphore_wait(barrier, NW - 1 + NY - 1 + 1)
     send_queries(0)
+    for load in loads[STEPS:]:
+        load.start()
     dispatch(1)
     send_queries(1)
     dispatch(2)
+    send_queries(2)
     dispatch(3)
 
-    tall_sub = lax.broadcasted_iota(I32, (ROWS, REQ), 0)
-    tall_lane = lax.broadcasted_iota(I32, (ROWS, REQ), 1)
+    tall_sub = lax.broadcasted_iota(I32, (HALF, REQ), 0)
+    tall_lane = lax.broadcasted_iota(I32, (HALF, REQ), 1)
     key_col = jnp.sum(
         jnp.where(lax.bitwise_and(tall_sub, REQ - 1) == tall_lane, slot, 0),
         axis=1, keepdims=True,
-    ) + 2 * lax.shift_right_logical(lax.broadcasted_iota(I32, (ROWS, 1), 0), 6)
-    slot_cols = lax.broadcasted_iota(I32, (ROWS, ROWS), 1)
-    for p in range(2):
-        hit = slot_cols == key_col - p * ROWS
-        gather[p] = jnp.where(hit, 1.0, 0.0).astype(BF16)
+    ) + 2 * lax.shift_right_logical(lax.broadcasted_iota(I32, (HALF, 1), 0), 6)
+    hit = lax.broadcasted_iota(I32, (HALF, ROWS), 1) == key_col
+    gather[...] = jnp.where(hit, 1.0, 0.0).astype(BF16)
     len_col[...] = jnp.broadcast_to(upright(len_ref[...]), (REQ, HD))
-    loads[1].wait()
-    loads[2].wait()
+    loads[4].wait()
+    loads[5].wait()
     vones[:, :, :HD] = pv[...]
     vones[:, :, HD:] = jnp.ones((2, PRE, HD), BF16)
 
-    for load in loads[3:7]:
+    for load in loads[6:10]:
         load.wait()
     qf[...] = q[...].astype(F32)
     nkf[...] = nk[...].astype(F32)
@@ -242,17 +247,24 @@
         def part(i, carry):
             some = pl.ds(i * PART, PART)
             logs = jnp.zeros((PART, 2 * HL, HD), F32)
+            arrived = q_recv[s, some].astype(F32)
+            results = []
             for p in range(2):
-                query = q_recv[s, some, :, p * HD:(p + 1) * HD].reshape(PART * 2 * HL, HD)
-                scores = dot_t(query, pk[p])
+                rows = slice(p * 8, p * 8 + 8)
+                query = jnp.concatenate([arrived[:, 0, rows], arrived[:, 1, rows]], axis=1)
+                scores = dot_t(query.astype(BF16).reshape(PART * 2 * HL, HD), pk[p])
                 top = jnp.max(scores, axis=-1, keepdims=True)
                 weights = jnp.exp2((scores - top) * (SCALE * LOG2E)).astype(BF16)
                 both = dot(weights, vones[p])
                 total = both[:, HD:]
-                result = (both[:, :HD] / total).astype(BF16)
-                r_send[s, some, :, p * HD:(p + 1) * HD] = result.reshape(PART, 2 * HL, HD)
+                results.append((both[:, :HD] / total).reshape(PART, 2 * HL, HD))
                 log = (top * SCALE + jnp.log(total)).reshape(PART, 2 * HL, HD)
                 logs = jnp.where(log_lane == place + p * 2 * HL, log, logs)
+            for half in range(2):
+                rows = slice(half * 8, half * 8 + 8)
+                r_send[s, some, half] = jnp.concatenate(
+                    [results[0][:, rows], results[1][:, rows]], axis=1
+                ).astype(BF16)
             l_send[s, some] = jnp.sum(logs, axis=1, keepdims=True)
             return carry
 
@@ -260,12 +272,14 @@
         r_recv[s, 0] = r_send[s, 0]
         l_recv[s, 0] = l_send[s, 0]
         send_logs(s)
-        send_results(s)
-
-    own = jnp.broadcast_to(
-        lax.bitwise_and(lax.shift_right_logical(slot_col, 4), NW - 1), (REQ, HD)
-    )
-    pick = lax.shift_right_logical(slot_col, 9) * (2 * HL) + lax.bitwise_and(slot_col, 1)
+        if s == LAST:
+            send_results(s, 0)
+            send_results(s, 1)
+        else:
+            send_results(s)
+
+    own = jnp.broadcast_to(lax.shift_right_logical(slot_col, 4), (REQ, HD))
+    pick = lax.bitwise_and(slot_col, 8) * 2 + lax.bitwise_and(slot_col, 1)
     lanes = lax.broadcasted_iota(I32, (REQ, HD), 1)
 
     def merge(s):
@@ -280,32 +294,47 @@
             a, b = jnp.exp(pre - high), jnp.exp(loc - high)
             pre_part[h] = a / (a + b)
             loc_out[s, h] = loc_out[s, h] * (b / (a + b))
-        await_all(r_recv.at[s, pl.ds(1, NW - 1)], rr.at[s])
-        back = dot(gather[0], r_recv[s, :, :, :HD].reshape(ROWS, HD)) + dot(
-            gather[1], r_recv[s, :, :, HD:].reshape(ROWS, HD)
-        )
-        for h in range(HL):
-            joint = pre_part[h] * back[h * REQ:(h + 1) * REQ] + loc_out[s, h]
+
+    def take(s, half):
+        back = dot(gather[...], r_recv[s, :, half].reshape(ROWS, HD))
+        for n in range(4):
+            h = half * 4 + n
+            joint = pre_part[h] * back[n * REQ:(n + 1) * REQ] + loc_out[s, h]
             attn[s, :, h * HD:(h + 1) * HD] = joint.astype(BF16)
 
     def block(dy, core):
         return lax.rem(y + dy, NY) * 2 + core
 
+    WIDE = HL * HD // 2
+
+    def term(s, dy, side):
+        n = block(dy, 1 - c if side else c)
+        if s == LAST:
+            return early[dy, side] + dot(attn[s, :, WIDE:], w[n, WIDE:])
+        return dot(attn[s], w[n])
+
+    def begin(s):
+        for side in (1, 0):
+            for dy in (2, 1, 3, 0):
+                n = block(dy, 1 - c if side else c)
+                early[dy, side] = dot(attn[s, :, :WIDE], w[n, :WIDE])
+
     def give(s, dy):
-        given[s, dy] = dot(attn[s], w[block(dy, 1 - c)]).astype(BF16)
+        given[s, dy] = term(s, dy, 1).astype(BF16)
         pltpu.make_async_remote_copy(
             src_ref=given.at[s, dy], dst_ref=c_recv.at[s, dy], send_sem=cs.at[s, dy],
             recv_sem=cr.at[s, dy], device_id=other, device_id_type=MESH,
         ).start()
 
     def keep(s, dy):
-        kept[s, dy] = dot(attn[s], w[block(dy, c)])
+        kept[s, dy] = term(s, dy, 0)
 
     def pair(s, dy):
         await_all(c_recv.at[s, dy], cr.at[s, dy])
         both = kept[s, dy] + c_recv[s, dy].astype(F32)
         if dy == 0:
             kept[s, dy] = both
+            pltpu.make_async_copy(kept.at[s, dy], own_hbm.at[s], out_sems.at[s]).start()
             return
         y_send[s, dy - 1] = both.astype(BF16)
         pltpu.make_async_remote_copy(
@@ -327,43 +356,45 @@
         keep(s, 0)
         pair(s, 0)
 
-    def finish(s):
-        await_all(y_recv.at[s], yr.at[s])
-        total = kept[s, 0]
-        for dy in range(NY - 1):
-            total = total + y_recv[s, dy].astype(F32)
-        out_v[s] = total.astype(BF16)
-        pltpu.make_async_copy(out_v.at[s], out_hbm.at[s], out_sems.at[s]).start()
+    def step(s):
+        merge(s)
+        if s == LAST:
+            for half in range(2):
+                await_all(r_recv.at[s, pl.ds(1, NW - 1), half], rr.at[s + half])
+                take(s, half)
+                if half == 0:
+                    begin(s)
+        else:
+            await_all(r_recv.at[s, pl.ds(1, NW - 1)], rr.at[s])
+            take(s, 0)
+            take(s, 1)
+        project(s)
 
     attend(0)
-    send_queries(2)
+    send_queries(3)
     attend(1)
-    send_queries(3)
-    for load in loads[7:]:
+    attend(2)
+    for load in loads[10:]:
         load.wait()
-    merge(0)
-    project(0)
-    attend(2)
-    merge(1)
-    project(1)
-    finish(0)
+    step(0)
     attend(3)
-    merge(2)
-    project(2)
-    finish(1)
-    merge(3)
-    project(3)
-    finish(2)
-    finish(3)
+    for s in range(1, STEPS):
+        step(s)
 
     for s in range(STEPS):
         await_all(q_send.at[s, pl.ds(1, NW - 1)], qs.at[s])
-        await_all(r_send.at[s, pl.ds(1, NW - 1)], rs.at[s])
+        if s == LAST:
+            for half in range(2):
+                await_all(r_send.at[s, pl.ds(1, NW - 1), half], rs.at[s + half])
+        else:
+            await_all(r_send.at[s, pl.ds(1, NW - 1)], rs.at[s])
         await_all(l_send.at[s, pl.ds(1, NW - 1)], ls.at[s])
         for dy in range(NY):
             await_all(given.at[s, dy], cs.at[s, dy])
         await_all(y_send.at[s], ys.at[s])
-        pltpu.make_async_copy(out_v.at[s], out_hbm.at[s], out_sems.at[s]).wait()
+        pltpu.make_async_copy(kept.at[s, 0], own_hbm.at[s], out_sems.at[s]).wait()
+    for s in range(STEPS):
+        await_all(y_recv.at[s], yr.at[s])
 
 
 def body(
@@ -373,13 +404,16 @@
     anywhere = pl.BlockSpec(memory_space=pl.ANY)
     vmem = pl.BlockSpec(memory_space=pltpu.VMEM)
     dma = pltpu.SemaphoreType.DMA
-    slots = (STEPS, NW, 2 * HL, 2 * HD)
+    slots = (STEPS, NW, 2, 16, HD)
     logs = (STEPS, NW, 1, HD)
-    return pl.pallas_call(
+    own, parts = pl.pallas_call(
         kernel,
-        out_shape=jax.ShapeDtypeStruct((STEPS, REQ, SHARE), BF16),
+        out_shape=(
+            jax.ShapeDtypeStruct((STEPS, REQ, SHARE), F32),
+            jax.ShapeDtypeStruct((STEPS, NY - 1, REQ, SHARE), BF16),
+        ),
         in_specs=[anywhere, vmem, vmem] + [anywhere] * 7,
-        out_specs=anywhere,
+        out_specs=(anywhere, anywhere),
         scratch_shapes=[
             pltpu.VMEM(queries.shape, BF16),
             pltpu.VMEM(new_keys.shape, BF16),
@@ -396,8 +430,8 @@
             pltpu.VMEM((LKEYS + HD, HD), BF16),
             pltpu.VMEM((LKEYS + HD, 2 * HD), BF16),
             pltpu.VMEM((REQ, HD), I32),
-            pltpu.VMEM((2, ROWS, ROWS), BF16),
-            pltpu.VMEM((2, ROWS, ROWS), BF16),
+            pltpu.VMEM((ROWS, HALF), BF16),
+            pltpu.VMEM((HALF, ROWS), BF16),
             pltpu.VMEM(slots, BF16),
             pltpu.VMEM(slots, BF16),
             pltpu.VMEM(slots, BF16),
@@ -408,15 +442,14 @@
             pltpu.VMEM((STEPS, HL, REQ, HD), F32),
             pltpu.VMEM((HL, REQ, HD), F32),
             pltpu.VMEM((STEPS, REQ, HL * HD), BF16),
+            pltpu.VMEM((NY, 2, REQ, SHARE), F32),
             pltpu.VMEM((STEPS, NY, REQ, SHARE), F32),
             pltpu.VMEM((STEPS, NY, REQ, SHARE), BF16),
             pltpu.VMEM((STEPS, NY, REQ, SHARE), BF16),
             pltpu.VMEM((STEPS, NY - 1, REQ, SHARE), BF16),
-            pltpu.VMEM((STEPS, NY - 1, REQ, SHARE), BF16),
-            pltpu.VMEM((STEPS, REQ, SHARE), BF16),
-            dma((7 + 2 * NY,)),
+            dma((STEPS + 6 + 2 * NY,)),
             dma((STEPS,)),
-        ] + [dma((STEPS,))] * 6 + [dma((STEPS, NY))] * 2 + [dma((STEPS,))] * 2,
+        ] + [dma((STEPS,))] * 2 + [dma((STEPS + 1,))] * 2 + [dma((STEPS,))] * 2 + [dma((STEPS, NY))] * 2 + [dma((STEPS,))] * 2,
         compiler_params=pltpu.CompilerParams(
             collective_id=0, has_side_effects=True, vmem_limit_bytes=62 * 2**20
         ),
@@ -425,6 +458,9 @@
         queries, prefix_of.reshape(1, REQ), suffix_len.reshape(1, REQ), new_keys, new_values,
         suffix_keys, suffix_values, prefix_keys, prefix_values, out_weight,
     )
+    for dy in range(NY - 1):
+        own = own + parts[:, dy].astype(F32)
+    return own.astype(BF16)
 
 
 def solution(mesh):

time: 74.3 us -> 71.9 us (0.968)
  Pallas kernels: 72.5 us -> 69.7 us
  other arithmetic: 0 us -> 2.11 us
  local copies, waits for them, and re-layouts: 1.67 us -> 0 us
    pallas_call x1, Pallas kernels: 72.5 us -> 69.7 us  [body(): pl.pallas_call(kernel, out_shape=(jax.ShapeDtypeStruct((STEPS, REQ, SHARE...]
    convert_element_type x0 -> x1, other arithmetic: none -> 2.11 us  [body(): return own.astype(BF16)]
    unnamed x1 -> x0, local copies, waits for them, and re-layouts: 1.67 us -> none
where the time goes in v3:
time: 71.9 us; the launch traced here: 71.8 us
  Pallas kernels  69.7 us (97%)
  other arithmetic  2.11 us (3%)
    pallas_call x1, Pallas kernels, body(): pl.pallas_call(kernel, out_shape=(jax.ShapeDtypeStruct((STEPS, REQ, SHARE...  69.7 us
    convert_element_type x1, other arithmetic, body(): return own.astype(BF16)  2.11 us

profile of v3, /device:TPU:1, one launch (start us, length us, event | category | flops | bytes accessed | tf_op | source)
XLA Modules:
  0.0 71.8 jit_solution(7436307085639774554)
XLA Ops:
  0.0 69.7 %attention.1 = (f32[4,64,512]{2,1,0:T(8,128)}, bf16[4,3,64,512]{3,2,1,0:T(8,128)(2,1)}) custom-call(bf16[4,64,1024]{2,1,0:T(8,128)(2,1)} %q_hbm.1, s32[1,64]{1,0:T(1,128)} %bitcast.15, s32[1,64]{1,0:T(1,128)} %bitcast.16, bf16[4,64,128]{2,1,0:T(8,128)(2,1)} %nk_hbm.1, bf16[4,64,128]{2,1,0:T(8,128)(2,1)} %nv_hbm.1, bf16[64,64,128]{2,1,0:T(8,128)(2,1)} %sk_hbm.1, ...), custom_call_target="tpu_custom_call" | custom-call | tf_op jit(solution)/shard_map/attention/pallas_call | solution.py:409
  69.7 2.1 %fusion = bf16[4,64,512]{2,1,0:T(8,128)(2,1)} fusion(f32[4,64,512]{2,1,0:T(8,128)} %get-tuple-element.7, bf16[4,3,64,512]{3,2,1,0:T(8,128)(2,1)} %get-tuple-element.8), kind=kLoop, calls=%fused_computation.1 | loop fusion | flops 917504 | bytes 1572864 | tf_op jit(solution)/shard_map/convert_element_type | solution.py:463

commit v4 on v3

--- a/solution.py
+++ b/solution.py
@@ -16,6 +16,8 @@
 ROWS = HL * REQ
 HALF = ROWS // 2
 LAST = STEPS - 1
+EARLY = 2
+FIRST = 1
 SCALE = HD ** (-0.5)
 LOG2E = 1.4426950408889634
 BLOCK = 8
@@ -25,6 +27,10 @@
 F32, BF16, I32 = jnp.float32, jnp.bfloat16, jnp.int32
 
 
+def is_early(s):
+    return FIRST <= s < FIRST + EARLY
+
+
 def dot(a, b):
     return lax.dot_general(a, b, (((1,), (0,)), ((), ())), preferred_element_type=F32)
 
@@ -40,7 +46,9 @@
     len_col,
     spread, gather, q_send, q_recv, r_send, r_recv, l_send, l_recv,
     loc_out, loc_log, pre_part, attn, early, kept, given, c_recv, y_send,
-    in_sems, out_sems, qs, qr, rs, rr, ls, lr, cs, cr, ys, yr,
+    order_in, order_out, pick_out, f_send, f_recv, raw, slot_attn, kept_e, given_e, c_recv_e,
+    y_send_e, y_recv_e, p_send, p_recv, own_v,
+    in_sems, out_sems, qs, qr, rs, rr, ls, lr, cs, cr, ys, yr, fs, fr, cse, cre, yse, yre, ps, pr,
 ):
     me_w, me_t = lax.axis_index("wide"), lax.axis_index("tensor")
     z, x = me_w // NX, me_w % NX
@@ -110,7 +118,8 @@
     spread[...] = jnp.where(hit, 1.0, 0.0).astype(BF16)
 
     def dispatch(s):
-        loads[s].wait()
+        if s < 2:
+            loads[s].wait()
         for half in range(2):
             stacked = jnp.concatenate(
                 [q[s, :, h * HD:(h + 1) * HD] for h in range(half * 4, half * 4 + 4)], axis=0
@@ -146,6 +155,30 @@
 
         lax.fori_loop(1, NW, one, 0)
 
+    def send_early_logs():
+        def one(i, carry):
+            dz, dx = offset(NW - i)
+            o = dz * NX + dx
+            pltpu.make_async_remote_copy(
+                src_ref=f_send.at[o], dst_ref=f_recv.at[o], send_sem=fs,
+                recv_sem=fr, device_id=ahead(dz, dx), device_id_type=MESH,
+            ).start()
+            return carry
+
+        lax.fori_loop(1, NW, one, 0)
+
+    def send_projected(s):
+        def one(i, carry):
+            dz, dx = offset(NW - i)
+            o = dz * NX + dx
+            pltpu.make_async_remote_copy(
+                src_ref=p_send.at[s, o], dst_ref=p_recv.at[s, o], send_sem=ps.at[s],
+                recv_sem=pr.at[s], device_id=behind(dz, dx), device_id_type=MESH,
+            ).start()
+            return carry
+
+        lax.fori_loop(1, NW, one, 0)
+
     def send_logs(s):
         def one(i, carry):
             dz, dx = offset(NW - i)
@@ -168,26 +201,12 @@
         load.start()
     dispatch(1)
     send_queries(1)
-    dispatch(2)
-    send_queries(2)
-    dispatch(3)
-
-    tall_sub = lax.broadcasted_iota(I32, (HALF, REQ), 0)
-    tall_lane = lax.broadcasted_iota(I32, (HALF, REQ), 1)
-    key_col = jnp.sum(
-        jnp.where(lax.bitwise_and(tall_sub, REQ - 1) == tall_lane, slot, 0),
-        axis=1, keepdims=True,
-    ) + 2 * lax.shift_right_logical(lax.broadcasted_iota(I32, (HALF, 1), 0), 6)
-    hit = lax.broadcasted_iota(I32, (HALF, ROWS), 1) == key_col
-    gather[...] = jnp.where(hit, 1.0, 0.0).astype(BF16)
+
     len_col[...] = jnp.broadcast_to(upright(len_ref[...]), (REQ, HD))
-    loads[4].wait()
-    loads[5].wait()
-    vones[:, :, :HD] = pv[...]
-    vones[:, :, HD:] = jnp.ones((2, PRE, HD), BF16)
-
     for load in loads[6:10]:
         load.wait()
+    loads[2].wait()
+    loads[3].wait()
     qf[...] = q[...].astype(F32)
     nkf[...] = nk[...].astype(F32)
     nvf[...] = nv[...].astype(F32)
@@ -237,6 +256,63 @@
 
     lax.fori_loop(0, REQ // BLOCK, local_block, 0)
 
+    own = jnp.broadcast_to(lax.shift_right_logical(slot_col, 4), (REQ, HD))
+    pick = lax.bitwise_and(slot_col, 8) * 2 + lax.bitwise_and(slot_col, 1)
+    lanes = lax.broadcasted_iota(I32, (REQ, HD), 1)
+
+    logs_out = jnp.zeros((REQ, HD), F32)
+    for e in range(EARLY):
+        for h in range(HL):
+            logs_out = jnp.where(lanes == pick + (e * 32 + 2 * h), loc_log[FIRST + e, h], logs_out)
+    for o in range(NW):
+        row = jnp.sum(jnp.where(own == o, logs_out, 0.0), axis=0, keepdims=True)
+        f_send[o] = row
+        if o == 0:
+            f_recv[o] = row
+    send_early_logs()
+    dispatch(2)
+    send_queries(2)
+    dispatch(3)
+    send_queries(3)
+
+    tall_sub = lax.broadcasted_iota(I32, (HALF, REQ), 0)
+    tall_lane = lax.broadcasted_iota(I32, (HALF, REQ), 1)
+    key_col = jnp.sum(
+        jnp.where(lax.bitwise_and(tall_sub, REQ - 1) == tall_lane, slot, 0),
+        axis=1, keepdims=True,
+    ) + 2 * lax.shift_right_logical(lax.broadcasted_iota(I32, (HALF, 1), 0), 6)
+    hit = lax.broadcasted_iota(I32, (HALF, ROWS), 1) == key_col
+    gather[...] = jnp.where(hit, 1.0, 0.0).astype(BF16)
+    slot_out = (
+        lax.shift_left(lax.shift_right_logical(slot, 4), 4)
+        + lax.shift_right_logical(lax.bitwise_and(slot, 8), 2) + lax.bitwise_and(slot, 1)
+    )
+    key_out = jnp.sum(
+        jnp.where(lax.bitwise_and(tall_sub, REQ - 1) == tall_lane, slot_out, 0),
+        axis=1, keepdims=True,
+    ) + 4 * lax.shift_right_logical(lax.broadcasted_iota(I32, (HALF, 1), 0), 6)
+    hit = lax.broadcasted_iota(I32, (HALF, ROWS), 1) == key_out
+    pick_out[...] = jnp.where(hit, 1.0, 0.0).astype(BF16)
+    at = lax.broadcasted_iota(I32, (ROWS, 1), 0)
+    column = lax.broadcasted_iota(I32, (ROWS, ROWS), 1)
+    turn = lax.bitwise_and(at, 1)
+    target = (
+        lax.bitwise_and(lax.shift_right_logical(at, 1), NW - 1) * 16
+        + lax.shift_right_logical(at, 6) * 2 + turn
+    )
+    order_in[...] = jnp.where(column == target, 1.0, 0.0).astype(BF16)
+    target = (
+        lax.bitwise_and(lax.shift_right_logical(at, 2), 3) * 128
+        + lax.bitwise_and(lax.shift_right_logical(at, 1), 1) * 64
+        + lax.shift_right_logical(at, 4) * 2 + turn
+    )
+    order_out[...] = jnp.where(column == target, 1.0, 0.0).astype(BF16)
+    loads[4].wait()
+    loads[5].wait()
+    vones[:, :, :HD] = pv[...]
+    vones[:, :, HD:] = jnp.ones((2, PRE, HD), BF16)
+
+
     log_lane = lax.broadcasted_iota(I32, (1, 2 * HL, HD), 2)
     place = lax.broadcasted_iota(I32, (1, 2 * HL, HD), 1)
     PART = 16
@@ -257,10 +333,19 @@
                 weights = jnp.exp2((scores - top) * (SCALE * LOG2E)).astype(BF16)
                 both = dot(weights, vones[p])
                 total = both[:, HD:]
-                results.append((both[:, :HD] / total).reshape(PART, 2 * HL, HD))
+                result = (both[:, :HD] / total).reshape(PART, 2 * HL, HD)
                 log = (top * SCALE + jnp.log(total)).reshape(PART, 2 * HL, HD)
+                if is_early(s):
+                    there = jnp.where(
+                        log_lane == place + ((s - FIRST) * 32 + p * 2 * HL), f_recv[some], 0.0
+                    )
+                    there = jnp.sum(there, axis=-1, keepdims=True)
+                    high = jnp.maximum(log, there)
+                    a, b = jnp.exp(log - high), jnp.exp(there - high)
+                    raw[p, some] = (result * (a / (a + b))).astype(BF16)
+                results.append(result)
                 logs = jnp.where(log_lane == place + p * 2 * HL, log, logs)
-            for half in range(2):
+            for half in range(0 if is_early(s) else 2):
                 rows = slice(half * 8, half * 8 + 8)
                 r_send[s, some, half] = jnp.concatenate(
                     [results[0][:, rows], results[1][:, rows]], axis=1
@@ -269,18 +354,20 @@
             return carry
 
         lax.fori_loop(0, NW // PART, part, 0)
-        r_recv[s, 0] = r_send[s, 0]
         l_recv[s, 0] = l_send[s, 0]
         send_logs(s)
+        if is_early(s):
+            for p in range(2):
+                moved = dot(order_in[...], raw[p].reshape(ROWS, HD)).astype(BF16)
+                for h in range(HL):
+                    slot_attn[p, :, h * HD:(h + 1) * HD] = moved[h * REQ:(h + 1) * REQ]
+            return
+        r_recv[s, 0] = r_send[s, 0]
         if s == LAST:
             send_results(s, 0)
             send_results(s, 1)
         else:
             send_results(s)
-
-    own = jnp.broadcast_to(lax.shift_right_logical(slot_col, 4), (REQ, HD))
-    pick = lax.bitwise_and(slot_col, 8) * 2 + lax.bitwise_and(slot_col, 1)
-    lanes = lax.broadcasted_iota(I32, (REQ, HD), 1)
 
     def merge(s):
         await_all(l_recv.at[s, pl.ds(1, NW - 1)], lr.at[s])
@@ -292,8 +379,12 @@
             loc = loc_log[s, h]
             high = jnp.maximum(pre, loc)
             a, b = jnp.exp(pre - high), jnp.exp(loc - high)
-            pre_part[h] = a / (a + b)
-            loc_out[s, h] = loc_out[s, h] * (b / (a + b))
+            mine = loc_out[s, h] * (b / (a + b))
+            if is_early(s):
+                attn[s, :, h * HD:(h + 1) * HD] = mine.astype(BF16)
+            else:
+                pre_part[h] = a / (a + b)
+                loc_out[s, h] = mine
 
     def take(s, half):
         back = dot(gather[...], r_recv[s, :, half].reshape(ROWS, HD))
@@ -338,7 +429,7 @@
             return
         y_send[s, dy - 1] = both.astype(BF16)
         pltpu.make_async_remote_copy(
-            src_ref=y_send.at[s, dy - 1], dst_ref=y_recv.at[s, dy - 1],
+            src_ref=y_send.at[s, dy - 1], dst_ref=y_recv.at[dy - 1, s],
             send_sem=ys.at[s], recv_sem=yr.at[s], device_id=across(dy), device_id_type=MESH,
         ).start()
 
@@ -356,6 +447,69 @@
         keep(s, 0)
         pair(s, 0)
 
+    def rows_of(u):
+        if u < EARLY:
+            return slot_attn[...].reshape(2 * REQ, HL * HD)
+        return attn[FIRST:FIRST + EARLY].reshape(2 * REQ, HL * HD)
+
+    def give_early(u, dy):
+        term = dot(rows_of(u), w[block(dy, 1 - c)]).astype(BF16)
+        given_e[u, dy] = term.reshape(2, REQ, SHARE)
+        pltpu.make_async_remote_copy(
+            src_ref=given_e.at[u, dy], dst_ref=c_recv_e.at[u, dy], send_sem=cse.at[u, dy],
+            recv_sem=cre.at[u, dy], device_id=other, device_id_type=MESH,
+        ).start()
+
+    def keep_early(u, dy):
+        kept_e[u, dy] = dot(rows_of(u), w[block(dy, c)]).reshape(2, REQ, SHARE)
+
+    def pair_early(u, dy):
+        await_all(c_recv_e.at[u, dy], cre.at[u, dy])
+        both = kept_e[u, dy] + c_recv_e[u, dy].astype(F32)
+        if dy == 0:
+            kept_e[u, dy] = both
+            return
+        y_send_e[u, dy - 1] = both.astype(BF16)
+        target = y_recv_e.at[u, dy - 1] if u < EARLY else y_recv.at[dy - 1, pl.ds(FIRST, EARLY)]
+        pltpu.make_async_remote_copy(
+            src_ref=y_send_e.at[u, dy - 1], dst_ref=target, send_sem=yse.at[u],
+            recv_sem=yre.at[u], device_id=across(dy), device_id_type=MESH,
+        ).start()
+
+    def project_early(u):
+        give_early(u, 2)
+        give_early(u, 1)
+        give_early(u, 3)
+        keep_early(u, 2)
+        keep_early(u, 1)
+        pair_early(u, 2)
+        keep_early(u, 3)
+        pair_early(u, 1)
+        give_early(u, 0)
+        pair_early(u, 3)
+        keep_early(u, 0)
+        pair_early(u, 0)
+
+    def return_early(s):
+        await_all(y_recv_e.at[s], yre.at[s])
+        total = kept_e[s, 0]
+        for dy in range(NY - 1):
+            total = total + y_recv_e[s, dy].astype(F32)
+        total = total.astype(BF16).reshape(2 * REQ, SHARE)
+        stacked = jnp.concatenate([total[:, j * HD:(j + 1) * HD] for j in range(4)], axis=0)
+        placed = dot(order_out[...], stacked).astype(BF16).reshape(NW, 16, HD)
+        p_send[s] = placed
+        p_recv[s, 0] = placed[0]
+        send_projected(s)
+
+    def combine_early(s):
+        await_all(p_recv.at[s, pl.ds(1, NW - 1)], pr.at[s])
+        back = dot(pick_out[...], p_recv[s].reshape(ROWS, HD))
+        for j in range(4):
+            cols = slice(j * HD, (j + 1) * HD)
+            own_v[s, :, cols] = kept_e[EARLY, 0, s, :, cols] + back[j * REQ:(j + 1) * REQ]
+        pltpu.make_async_copy(own_v.at[s], own_hbm.at[FIRST + s], out_sems.at[FIRST + s]).start()
+
     def step(s):
         merge(s)
         if s == LAST:
@@ -371,30 +525,50 @@
         project(s)
 
     attend(0)
-    send_queries(3)
+    await_all(f_recv.at[pl.ds(1, NW - 1)], fr)
     attend(1)
-    attend(2)
     for load in loads[10:]:
         load.wait()
+    project_early(0)
+    attend(2)
+    project_early(1)
+    return_early(0)
+    attend(3)
+    merge(1)
+    merge(2)
+    project_early(2)
     step(0)
-    attend(3)
-    for s in range(1, STEPS):
-        step(s)
-
+    return_early(1)
+    combine_early(0)
+    step(3)
+    combine_early(1)
+
+    await_all(f_send.at[pl.ds(1, NW - 1)], fs)
+    for u in range(EARLY + 1):
+        for dy in range(NY):
+            await_all(given_e.at[u, dy], cse.at[u, dy])
+        await_all(y_send_e.at[u], yse.at[u])
+    await_all(y_recv.at[:, pl.ds(FIRST, EARLY)], yre.at[EARLY])
+    for s in range(EARLY):
+        await_all(p_send.at[s, pl.ds(1, NW - 1)], ps.at[s])
+        pltpu.make_async_copy(own_v.at[s], own_hbm.at[FIRST + s], out_sems.at[FIRST + s]).wait()
     for s in range(STEPS):
         await_all(q_send.at[s, pl.ds(1, NW - 1)], qs.at[s])
+        await_all(l_send.at[s, pl.ds(1, NW - 1)], ls.at[s])
+        if is_early(s):
+            continue
         if s == LAST:
             for half in range(2):
                 await_all(r_send.at[s, pl.ds(1, NW - 1), half], rs.at[s + half])
         else:
             await_all(r_send.at[s, pl.ds(1, NW - 1)], rs.at[s])
-        await_all(l_send.at[s, pl.ds(1, NW - 1)], ls.at[s])
         for dy in range(NY):
             await_all(given.at[s, dy], cs.at[s, dy])
         await_all(y_send.at[s], ys.at[s])
         pltpu.make_async_copy(kept.at[s, 0], own_hbm.at[s], out_sems.at[s]).wait()
     for s in range(STEPS):
-        await_all(y_recv.at[s], yr.at[s])
+        if not is_early(s):
+            await_all(y_recv.at[:, s], yr.at[s])
 
 
 def body(
@@ -410,7 +584,7 @@
         kernel,
         out_shape=(
             jax.ShapeDtypeStruct((STEPS, REQ, SHARE), F32),
-            jax.ShapeDtypeStruct((STEPS, NY - 1, REQ, SHARE), BF16),
+            jax.ShapeDtypeStruct((NY - 1, STEPS, REQ, SHARE), BF16),
         ),
         in_specs=[anywhere, vmem, vmem] + [anywhere] * 7,
         out_specs=(anywhere, anywhere),
@@ -447,9 +621,25 @@
             pltpu.VMEM((STEPS, NY, REQ, SHARE), BF16),
             pltpu.VMEM((STEPS, NY, REQ, SHARE), BF16),
             pltpu.VMEM((STEPS, NY - 1, REQ, SHARE), BF16),
+            pltpu.VMEM((ROWS, ROWS), BF16),
+            pltpu.VMEM((ROWS, ROWS), BF16),
+            pltpu.VMEM((HALF, ROWS), BF16),
+            pltpu.VMEM((NW, 1, HD), F32),
+            pltpu.VMEM((NW, 1, HD), F32),
+            pltpu.VMEM((2, NW, 16, HD), BF16),
+            pltpu.VMEM((2, REQ, HL * HD), BF16),
+            pltpu.VMEM((EARLY + 1, NY, 2, REQ, SHARE), F32),
+            pltpu.VMEM((EARLY + 1, NY, 2, REQ, SHARE), BF16),
+            pltpu.VMEM((EARLY + 1, NY, 2, REQ, SHARE), BF16),
+            pltpu.VMEM((EARLY + 1, NY - 1, 2, REQ, SHARE), BF16),
+            pltpu.VMEM((EARLY, NY - 1, 2, REQ, SHARE), BF16),
+            pltpu.VMEM((EARLY, NW, 16, HD), BF16),
+            pltpu.VMEM((EARLY, NW, 16, HD), BF16),
+            pltpu.VMEM((EARLY, REQ, SHARE), F32),
             dma((STEPS + 6 + 2 * NY,)),
             dma((STEPS,)),
-        ] + [dma((STEPS,))] * 2 + [dma((STEPS + 1,))] * 2 + [dma((STEPS,))] * 2 + [dma((STEPS, NY))] * 2 + [dma((STEPS,))] * 2,
+        ] + [dma((STEPS,))] * 2 + [dma((STEPS + 1,))] * 2 + [dma((STEPS,))] * 2 + [dma((STEPS, NY))] * 2 + [dma((STEPS,))] * 2
+        + [dma, dma] + [dma((EARLY + 1, NY))] * 2 + [dma((EARLY + 1,))] * 2 + [dma((EARLY,))] * 2,
         compiler_params=pltpu.CompilerParams(
             collective_id=0, has_side_effects=True, vmem_limit_bytes=62 * 2**20
         ),
@@ -459,7 +649,7 @@
         suffix_keys, suffix_values, prefix_keys, prefix_values, out_weight,
     )
     for dy in range(NY - 1):
-        own = own + parts[:, dy].astype(F32)
+        own = own + parts[dy].astype(F32)
     return own.astype(BF16)
 
 

time: 71.9 us -> 69.9 us (0.972)
  Pallas kernels: 69.7 us -> 67.6 us
    pallas_call x1, Pallas kernels: 69.7 us -> 67.6 us  [body(): pl.pallas_call(kernel, out_shape=(jax.ShapeDtypeStruct((STEPS, REQ, SHARE...]
where the time goes in v4:
time: 69.9 us; the launch traced here: 69.8 us
  Pallas kernels  67.6 us (97%)
  other arithmetic  2.11 us (3%)
    pallas_call x1, Pallas kernels, body(): pl.pallas_call(kernel, out_shape=(jax.ShapeDtypeStruct((STEPS, REQ, SHARE...  67.6 us
    convert_element_type x1, other arithmetic, body(): return own.astype(BF16)  2.11 us

profile of v4, /device:TPU:1, one launch (start us, length us, event | category | flops | bytes accessed | tf_op | source)
XLA Modules:
  0.0 69.8 jit_solution(13348008411574054655)
XLA Ops:
  0.0 67.6 %attention.1 = (f32[4,64,512]{2,1,0:T(8,128)}, bf16[3,4,64,512]{3,2,1,0:T(8,128)(2,1)}) custom-call(bf16[4,64,1024]{2,1,0:T(8,128)(2,1)} %q_hbm.1, s32[1,64]{1,0:T(1,128)} %bitcast.11, s32[1,64]{1,0:T(1,128)} %bitcast.12, bf16[4,64,128]{2,1,0:T(8,128)(2,1)} %nk_hbm.1, bf16[4,64,128]{2,1,0:T(8,128)(2,1)} %nv_hbm.1, bf16[64,64,128]{2,1,0:T(8,128)(2,1)} %sk_hbm.1, ...), custom_call_target="tpu_custom_call" | custom-call | tf_op jit(solution)/shard_map/attention/pallas_call | solution.py:583
  67.7 2.1 %fusion = bf16[4,64,512]{2,1,0:T(8,128)(2,1)} fusion(f32[4,64,512]{2,1,0:T(8,128)} %get-tuple-element.7, bf16[3,4,64,512]{3,2,1,0:T(8,128)(2,1)} %get-tuple-element.8), kind=kLoop, calls=%fused_computation.1 | loop fusion | flops 917504 | bytes 1572864 | tf_op jit(solution)/shard_map/convert_element_type | solution.py:653

commit v5 on v4

--- a/solution.py
+++ b/solution.py
@@ -40,10 +40,10 @@
 
 
 def kernel(
-    q_hbm, pof_ref, len_ref, nk_hbm, nv_hbm, sk_hbm, sv_hbm, pk_hbm, pv_hbm, w_hbm,
+    q_hbm, pof_hbm, len_hbm, nk_hbm, nv_hbm, sk_hbm, sv_hbm, pk_hbm, pv_hbm, w_hbm,
     own_hbm, y_recv,
     q, nk, nv, sk, sv, pk, pv, w, vones, qf, nkf, nvf, kloc, vloc,
-    len_col,
+    pof_ref, len_ref, len_col,
     spread, gather, q_send, q_recv, r_send, r_recv, l_send, l_recv,
     loc_out, loc_log, pre_part, attn, early, kept, given, c_recv, y_send,
     order_in, order_out, pick_out, f_send, f_recv, raw, slot_attn, kept_e, given_e, c_recv_e,
@@ -79,7 +79,11 @@
             + [(w_hbm.at[:, pl.ds(n * SHARE, SHARE)], w.at[n]) for n in range(2 * NY)]
         )
     ]
-    for load in loads[:STEPS]:
+    tables = [
+        pltpu.make_async_copy(src, dst, in_sems.at[len(loads) + n])
+        for n, (src, dst) in enumerate([(pof_hbm, pof_ref), (len_hbm, len_ref)])
+    ]
+    for load in tables + loads[:STEPS]:
         load.start()
 
     barrier = pltpu.get_barrier_semaphore()
@@ -93,6 +97,7 @@
         pl.semaphore_signal(barrier, inc=1, device_id=across(dy), device_id_type=MESH)
     pl.semaphore_signal(barrier, inc=1, device_id=other, device_id_type=MESH)
 
+    tables[0].wait()
     pof = pof_ref[...]
     sub = lax.broadcasted_iota(I32, (REQ, REQ), 0)
     lane = lax.broadcasted_iota(I32, (REQ, REQ), 1)
@@ -202,6 +207,7 @@
     dispatch(1)
     send_queries(1)
 
+    tables[1].wait()
     len_col[...] = jnp.broadcast_to(upright(len_ref[...]), (REQ, HD))
     for load in loads[6:10]:
         load.wait()
@@ -576,7 +582,7 @@
     prefix_keys, prefix_values, prefix_of, out_weight,
 ):
     anywhere = pl.BlockSpec(memory_space=pl.ANY)
-    vmem = pl.BlockSpec(memory_space=pltpu.VMEM)
+    fixed = functools.partial(pltpu.with_memory_space_constraint, memory_space=pltpu.HBM)
     dma = pltpu.SemaphoreType.DMA
     slots = (STEPS, NW, 2, 16, HD)
     logs = (STEPS, NW, 1, HD)
@@ -586,7 +592,7 @@
             jax.ShapeDtypeStruct((STEPS, REQ, SHARE), F32),
             jax.ShapeDtypeStruct((NY - 1, STEPS, REQ, SHARE), BF16),
         ),
-        in_specs=[anywhere, vmem, vmem] + [anywhere] * 7,
+        in_specs=[anywhere] * 10,
         out_specs=(anywhere, anywhere),
         scratch_shapes=[
             pltpu.VMEM(queries.shape, BF16),
@@ -603,6 +609,8 @@
             pltpu.VMEM(new_values.shape, F32),
             pltpu.VMEM((LKEYS + HD, HD), BF16),
             pltpu.VMEM((LKEYS + HD, 2 * HD), BF16),
+            pltpu.VMEM((1, REQ), I32),
+            pltpu.VMEM((1, REQ), I32),
             pltpu.VMEM((REQ, HD), I32),
             pltpu.VMEM((ROWS, HALF), BF16),
             pltpu.VMEM((HALF, ROWS), BF16),
@@ -636,17 +644,21 @@
             pltpu.VMEM((EARLY, NW, 16, HD), BF16),
             pltpu.VMEM((EARLY, NW, 16, HD), BF16),
             pltpu.VMEM((EARLY, REQ, SHARE), F32),
-            dma((STEPS + 6 + 2 * NY,)),
+            dma((STEPS + 8 + 2 * NY,)),
             dma((STEPS,)),
         ] + [dma((STEPS,))] * 2 + [dma((STEPS + 1,))] * 2 + [dma((STEPS,))] * 2 + [dma((STEPS, NY))] * 2 + [dma((STEPS,))] * 2
         + [dma, dma] + [dma((EARLY + 1, NY))] * 2 + [dma((EARLY + 1,))] * 2 + [dma((EARLY,))] * 2,
         compiler_params=pltpu.CompilerParams(
-            collective_id=0, has_side_effects=True, vmem_limit_bytes=62 * 2**20
+            collective_id=0, has_side_effects=True, vmem_limit_bytes=48 * 2**20
         ),
         name="attention",
     )(
-        queries, prefix_of.reshape(1, REQ), suffix_len.reshape(1, REQ), new_keys, new_values,
-        suffix_keys, suffix_values, prefix_keys, prefix_values, out_weight,
+        fixed(queries), fixed(prefix_of.reshape(1, REQ)), fixed(suffix_len.reshape(1, REQ)),
+        *(
+            fixed(a)
+            for a in (new_keys, new_values, suffix_keys, suffix_values,
+                      prefix_keys, prefix_values, out_weight)
+        ),
     )
     for dy in range(NY - 1):
         own = own + parts[dy].astype(F32)

time: 69.9 us -> 68.5 us (0.980)
  other arithmetic: 2.11 us -> 0.84 us
    convert_element_type x1, other arithmetic: 2.11 us -> 0.84 us  [body(): return own.astype(BF16)]
where the time goes in v5:
time: 68.5 us; the launch traced here: 68.4 us
  Pallas kernels  67.6 us (99%)
  other arithmetic  0.84 us (1%)
    pallas_call x1, Pallas kernels, body(): pl.pallas_call(kernel, out_shape=(jax.ShapeDtypeStruct((STEPS, REQ, SHARE...  67.6 us

profile of v5, /device:TPU:1, one launch (start us, length us, event | category | flops | bytes accessed | tf_op | source)
XLA Modules:
  0.0 68.4 jit_solution(7537857014682192159)
XLA Ops:
  0.0 67.6 %attention.1 = (f32[4,64,512]{2,1,0:T(8,128)S(1)}, bf16[3,4,64,512]{3,2,1,0:T(8,128)(2,1)S(1)}) custom-call(bf16[4,64,1024]{2,1,0:T(8,128)(2,1)} %q_hbm.1, s32[1,64]{1,0:T(1,128)} %bitcast.11, s32[1,64]{1,0:T(1,128)} %bitcast.12, bf16[4,64,128]{2,1,0:T(8,128)(2,1)} %nk_hbm.1, bf16[4,64,128]{2,1,0:T(8,128)(2,1)} %nv_hbm.1, bf16[64,64,128]{2,1,0:T(8,128)(2,1)} %sk_hbm.1, ...), custom_call_target="tpu_custom_call" | custom-call | tf_op jit(solution)/shard_map/attention/pallas_call | solution.py:589
  67.6 0.8 %fusion = bf16[4,64,512]{2,1,0:T(8,128)(2,1)} fusion(f32[4,64,512]{2,1,0:T(8,128)S(1)} %get-tuple-element.7, bf16[3,4,64,512]{3,2,1,0:T(8,128)(2,1)S(1)} %get-tuple-element.8), kind=kLoop, calls=%fused_computation.1 | loop fusion | flops 917504 | bytes 1572864 | tf_op jit(solution)/shard_map/convert_element_type | solution.py:665

commit v6 on v5

--- a/solution.py
+++ b/solution.py
@@ -45,7 +45,7 @@
     q, nk, nv, sk, sv, pk, pv, w, vones, qf, nkf, nvf, kloc, vloc,
     pof_ref, len_ref, len_col,
     spread, gather, q_send, q_recv, r_send, r_recv, l_send, l_recv,
-    loc_out, loc_log, pre_part, attn, early, kept, given, c_recv, y_send,
+    loc_out, loc_log, pre_part, attn, kept, given, c_recv, y_send,
     order_in, order_out, pick_out, f_send, f_recv, raw, slot_attn, kept_e, given_e, c_recv_e,
     y_send_e, y_recv_e, p_send, p_recv, own_v,
     in_sems, out_sems, qs, qr, rs, rr, ls, lr, cs, cr, ys, yr, fs, fr, cse, cre, yse, yre, ps, pr,
@@ -145,16 +145,13 @@
 
         lax.fori_loop(1, NW, one, 0)
 
-    def send_results(s, half=None):
-        part = pl.ds(0, 2) if half is None else pl.ds(half, 1)
-
+    def send_results(s):
         def one(i, carry):
             dz, dx = offset(NW - i)
             o = dz * NX + dx
             pltpu.make_async_remote_copy(
-                src_ref=r_send.at[s, o, part], dst_ref=r_recv.at[s, o, part],
-                send_sem=rs.at[s + (half or 0)], recv_sem=rr.at[s + (half or 0)],
-                device_id=behind(dz, dx), device_id_type=MESH,
+                src_ref=r_send.at[s, o], dst_ref=r_recv.at[s, o], send_sem=rs.at[s],
+                recv_sem=rr.at[s], device_id=behind(dz, dx), device_id_type=MESH,
             ).start()
             return carry
 
@@ -350,18 +347,22 @@
                     a, b = jnp.exp(log - high), jnp.exp(there - high)
                     raw[p, some] = (result * (a / (a + b))).astype(BF16)
                 results.append(result)
-                logs = jnp.where(log_lane == place + p * 2 * HL, log, logs)
+                logs = jnp.where(log_lane == place + (s * 32 + p * 2 * HL), log, logs)
             for half in range(0 if is_early(s) else 2):
                 rows = slice(half * 8, half * 8 + 8)
                 r_send[s, some, half] = jnp.concatenate(
                     [results[0][:, rows], results[1][:, rows]], axis=1
                 ).astype(BF16)
-            l_send[s, some] = jnp.sum(logs, axis=1, keepdims=True)
+            row = jnp.sum(logs, axis=1, keepdims=True)
+            if 0 < s < LAST:
+                row = row + l_send[0, some]
+            l_send[s // LAST, some] = row
             return carry
 
         lax.fori_loop(0, NW // PART, part, 0)
-        l_recv[s, 0] = l_send[s, 0]
-        send_logs(s)
+        if s >= LAST - 1:
+            l_recv[s // LAST, 0] = l_send[s // LAST, 0]
+            send_logs(s // LAST)
         if is_early(s):
             for p in range(2):
                 moved = dot(order_in[...], raw[p].reshape(ROWS, HD)).astype(BF16)
@@ -369,19 +370,17 @@
                     slot_attn[p, :, h * HD:(h + 1) * HD] = moved[h * REQ:(h + 1) * REQ]
             return
         r_recv[s, 0] = r_send[s, 0]
-        if s == LAST:
-            send_results(s, 0)
-            send_results(s, 1)
-        else:
-            send_results(s)
+        send_results(s)
 
     def merge(s):
-        await_all(l_recv.at[s, pl.ds(1, NW - 1)], lr.at[s])
+        g = s // LAST
+        if s in (FIRST, LAST):
+            await_all(l_recv.at[g, pl.ds(1, NW - 1)], lr.at[g])
         logs = jnp.zeros((REQ, HD), F32)
         for o in range(NW):
-            logs = jnp.where(own == o, l_recv[s, o], logs)
+            logs = jnp.where(own == o, l_recv[g, o], logs)
         for h in range(HL):
-            pre = jnp.sum(jnp.where(lanes == pick + 2 * h, logs, 0.0), axis=1, keepdims=True)
+            pre = jnp.sum(jnp.where(lanes == pick + (s * 32 + 2 * h), logs, 0.0), axis=1, keepdims=True)
             loc = loc_log[s, h]
             high = jnp.maximum(pre, loc)
             a, b = jnp.exp(pre - high), jnp.exp(loc - high)
@@ -402,19 +401,8 @@
     def block(dy, core):
         return lax.rem(y + dy, NY) * 2 + core
 
-    WIDE = HL * HD // 2
-
     def term(s, dy, side):
-        n = block(dy, 1 - c if side else c)
-        if s == LAST:
-            return early[dy, side] + dot(attn[s, :, WIDE:], w[n, WIDE:])
-        return dot(attn[s], w[n])
-
-    def begin(s):
-        for side in (1, 0):
-            for dy in (2, 1, 3, 0):
-                n = block(dy, 1 - c if side else c)
-                early[dy, side] = dot(attn[s, :, :WIDE], w[n, :WIDE])
+        return dot(attn[s], w[block(dy, 1 - c if side else c)])
 
     def give(s, dy):
         given[s, dy] = term(s, dy, 1).astype(BF16)
@@ -518,16 +506,9 @@
 
     def step(s):
         merge(s)
-        if s == LAST:
-            for half in range(2):
-                await_all(r_recv.at[s, pl.ds(1, NW - 1), half], rr.at[s + half])
-                take(s, half)
-                if half == 0:
-                    begin(s)
-        else:
-            await_all(r_recv.at[s, pl.ds(1, NW - 1)], rr.at[s])
-            take(s, 0)
-            take(s, 1)
+        await_all(r_recv.at[s, pl.ds(1, NW - 1)], rr.at[s])
+        take(s, 0)
+        take(s, 1)
         project(s)
 
     attend(0)
@@ -555,19 +536,16 @@
             await_all(given_e.at[u, dy], cse.at[u, dy])
         await_all(y_send_e.at[u], yse.at[u])
     await_all(y_recv.at[:, pl.ds(FIRST, EARLY)], yre.at[EARLY])
+    for g in range(2):
+        await_all(l_send.at[g, pl.ds(1, NW - 1)], ls.at[g])
     for s in range(EARLY):
         await_all(p_send.at[s, pl.ds(1, NW - 1)], ps.at[s])
         pltpu.make_async_copy(own_v.at[s], own_hbm.at[FIRST + s], out_sems.at[FIRST + s]).wait()
     for s in range(STEPS):
         await_all(q_send.at[s, pl.ds(1, NW - 1)], qs.at[s])
-        await_all(l_send.at[s, pl.ds(1, NW - 1)], ls.at[s])
         if is_early(s):
             continue
-        if s == LAST:
-            for half in range(2):
-                await_all(r_send.at[s, pl.ds(1, NW - 1), half], rs.at[s + half])
-        else:
-            await_all(r_send.at[s, pl.ds(1, NW - 1)], rs.at[s])
+        await_all(r_send.at[s, pl.ds(1, NW - 1)], rs.at[s])
         for dy in range(NY):
             await_all(given.at[s, dy], cs.at[s, dy])
         await_all(y_send.at[s], ys.at[s])
@@ -585,7 +563,7 @@
     fixed = functools.partial(pltpu.with_memory_space_constraint, memory_space=pltpu.HBM)
     dma = pltpu.SemaphoreType.DMA
     slots = (STEPS, NW, 2, 16, HD)
-    logs = (STEPS, NW, 1, HD)
+    logs = (2, NW, 1, HD)
     own, parts = pl.pallas_call(
         kernel,
         out_shape=(
@@ -624,7 +602,6 @@
             pltpu.VMEM((STEPS, HL, REQ, HD), F32),
             pltpu.VMEM((HL, REQ, HD), F32),
             pltpu.VMEM((STEPS, REQ, HL * HD), BF16),
-            pltpu.VMEM((NY, 2, REQ, SHARE), F32),
             pltpu.VMEM((STEPS, NY, REQ, SHARE), F32),
             pltpu.VMEM((STEPS, NY, REQ, SHARE), BF16),
             pltpu.VMEM((STEPS, NY, REQ, SHARE), BF16),
@@ -646,7 +623,7 @@
             pltpu.VMEM((EARLY, REQ, SHARE), F32),
             dma((STEPS + 8 + 2 * NY,)),
             dma((STEPS,)),
-        ] + [dma((STEPS,))] * 2 + [dma((STEPS + 1,))] * 2 + [dma((STEPS,))] * 2 + [dma((STEPS, NY))] * 2 + [dma((STEPS,))] * 2
+        ] + [dma((STEPS,))] * 6 + [dma((STEPS, NY))] * 2 + [dma((STEPS,))] * 2
         + [dma, dma] + [dma((EARLY + 1, NY))] * 2 + [dma((EARLY + 1,))] * 2 + [dma((EARLY,))] * 2,
         compiler_params=pltpu.CompilerParams(
             collective_id=0, has_side_effects=True, vmem_limit_bytes=48 * 2**20

time: 68.5 us -> 65.6 us (0.958)
  Pallas kernels: 67.6 us -> 64.7 us
    pallas_call x1, Pallas kernels: 67.6 us -> 64.7 us  [body(): pl.pallas_call(kernel, out_shape=(jax.ShapeDtypeStruct((STEPS, REQ, SHARE...]
where the time goes in v6:
time: 65.6 us
  Pallas kernels  64.7 us (99%)
  other arithmetic  0.84 us (1%)
    pallas_call x1, Pallas kernels, body(): pl.pallas_call(kernel, out_shape=(jax.ShapeDtypeStruct((STEPS, REQ, SHARE...  64.7 us

profile of v6, /device:TPU:1, one launch (start us, length us, event | category | flops | bytes accessed | tf_op | source)
XLA Modules:
  0.0 65.6 jit_solution(18284001522768988896)
XLA Ops:
  0.0 64.7 %attention.1 = (f32[4,64,512]{2,1,0:T(8,128)S(1)}, bf16[3,4,64,512]{3,2,1,0:T(8,128)(2,1)S(1)}) custom-call(bf16[4,64,1024]{2,1,0:T(8,128)(2,1)} %q_hbm.1, s32[1,64]{1,0:T(1,128)} %bitcast.11, s32[1,64]{1,0:T(1,128)} %bitcast.12, bf16[4,64,128]{2,1,0:T(8,128)(2,1)} %nk_hbm.1, bf16[4,64,128]{2,1,0:T(8,128)(2,1)} %nv_hbm.1, bf16[64,64,128]{2,1,0:T(8,128)(2,1)} %sk_hbm.1, ...), custom_call_target="tpu_custom_call" | custom-call | tf_op jit(solution)/shard_map/attention/pallas_call | solution.py:567
  64.7 0.8 %fusion = bf16[4,64,512]{2,1,0:T(8,128)(2,1)} fusion(f32[4,64,512]{2,1,0:T(8,128)S(1)} %get-tuple-element.7, bf16[3,4,64,512]{3,2,1,0:T(8,128)(2,1)S(1)} %get-tuple-element.8), kind=kLoop, calls=%fused_computation.1 | loop fusion | flops 917504 | bytes 1572864 | tf_op jit(solution)/shard_map/convert_element_type | solution.py:642
